TPU v7x, 32 devices: a whole 2x2x4 slice. The times are simulated.
32 devices in a mesh: dp: 2 (over x), section: 2 (over core), grid: 8 (over z, y).
Axes of the slice: x: 2, y: 2, z: 4, core: 2. Of those that a mesh axis runs over, the one named last changes fastest.
Arguments:
- section_edges: bfloat16 [2, 2, 16, 512, 768], P('section', None, ('dp', 'grid')), may hold values from -6 to 6
- lengths: int32 [2, 16], P(None, ('dp', 'grid')), may hold values from 128 to 512, as said below
- joint_weight: bfloat16 [2, 768, 2304], P('section', 'grid'), may hold values from -0.21875 to 0.21875
- query_bias: float32 [2, 768], P('section'), may hold values from -3 to 3
- value_bias: float32 [2, 768], P('section'), may hold values from -3 to 3
- output_weight: bfloat16 [2, 768, 768], P('section', 'grid'), may hold values from -1.75 to 1.75
- output_bias: float32 [2, 768], P('section'), may hold values from -2 to 2
- first_gain: float32 [2, 768], P('section'), may hold values from 0.25 to 1.75
- first_shift: float32 [2, 768], P('section'), may hold values from -2 to 2
- expand_weight: bfloat16 [2, 768, 3072], P('section', 'grid'), may hold values from -0.21875 to 0.21875
- expand_bias: float32 [2, 3072], P('section'), may hold values from -3 to 3
- reduce_weight: bfloat16 [2, 3072, 768], P('section', 'grid'), may hold values from -0.109375 to 0.109375
- reduce_bias: float32 [2, 768], P('section'), may hold values from -2 to 2
- second_gain: float32 [2, 768], P('section'), may hold values from 0.25 to 1.75
- second_shift: float32 [2, 768], P('section'), may hold values from -2 to 2
Outputs:
- boundary: float32 [2, 2, 16, 512, 768], P('section', None, ('dp', 'grid'))
- joint_weight_grad: float32 [2, 768, 2304], P('section', 'grid')
- query_bias_grad: float32 [2, 768], P('section')
- value_bias_grad: float32 [2, 768], P('section')
- output_weight_grad: float32 [2, 768, 768], P('section', 'grid')
- output_bias_grad: float32 [2, 768], P('section')
- first_gain_grad: float32 [2, 768], P('section')
- first_shift_grad: float32 [2, 768], P('section')
- expand_weight_grad: float32 [2, 768, 3072], P('section', 'grid')
- expand_bias_grad: float32 [2, 3072], P('section')
- reduce_weight_grad: float32 [2, 3072, 768], P('section', 'grid')
- reduce_bias_grad: float32 [2, 768], P('section')
- second_gain_grad: float32 [2, 768], P('section')
- second_shift_grad: float32 [2, 768], P('section')
Inputs may be any that keep to these rules, and one draw needn't show every extreme that they name: `lengths`: in each micro-batch one sequence has exactly 512 valid tokens and another exactly a quarter of 512.
All inputs are finite; a program needn't handle non-finite values.
Results may differ from a plain program's by a relative error of at most 0.017.
Values may be sent and summed in bfloat16 or wider, within the bound.
A program may use at most 256 MiB of HBM per device.

v0:
```python
from functools import partial
import math

import jax
import jax.numpy as jnp
from jax import lax
from jax.sharding import PartitionSpec as P

HEADS = 12


EPSILON = 1e-06
MASKED = -1000000000.0
LOWER = jnp.bfloat16
WIDE = jnp.float32


def from_behind(array, axis, by):
    length = lax.axis_size(axis)
    pairs = [(i, i + by) for i in range(length) if 0 <= i + by < length]
    return lax.ppermute(array, axis, pairs)


def norm_forward(residual, gain_vector, shift_vector):
    center = residual - jnp.mean(residual, axis=-1, keepdims=True)
    inverse = lax.rsqrt(jnp.mean(center * center, axis=-1, keepdims=True) + EPSILON)
    normed = center * inverse
    return (normed * gain_vector + shift_vector, normed, inverse)


def norm_backward(gradient, normed, inverse, gain_vector):
    scaled = gradient * gain_vector
    return inverse * (
        scaled
        - jnp.mean(scaled, axis=-1, keepdims=True)
        - normed * jnp.mean(scaled * normed, axis=-1, keepdims=True)
    )


def times_transposed(left_rows, right_rows):
    return lax.dot_general(
        left_rows, right_rows, (((1,), (1,)), ((), ())), preferred_element_type=WIDE
    )


def masked_scores(query_heads, key_heads, length):
    score_scale = query_heads.shape[-1] ** (-0.5)
    raw_scores = (
        jnp.einsum("qhe,khe->hqk", query_heads, key_heads, preferred_element_type=WIDE)
        * score_scale
    )
    places = lax.broadcasted_iota(jnp.int32, raw_scores.shape, 2)
    return jnp.where(places < length, raw_scores, MASKED)


def attend(pieces):
    query_heads, key_heads, value_heads, length = pieces
    scores = masked_scores(query_heads, key_heads, length)
    row_max = jnp.max(scores, axis=-1, keepdims=True)
    weights = jnp.exp(scores - row_max)
    row_total = jnp.sum(weights, axis=-1, keepdims=True)
    probabilities = (weights / row_total).astype(LOWER)
    attended = jnp.einsum("hqk,khe->qhe", probabilities, value_heads, preferred_element_type=WIDE)
    return (attended, row_max + jnp.log(row_total))


def attend_backward(pieces):
    query_heads, key_heads, value_heads, length, log_total, grad_attended = pieces
    score_scale = query_heads.shape[-1] ** (-0.5)
    scores = masked_scores(query_heads, key_heads, length)
    probabilities = jnp.exp(scores - log_total)
    grad_value = jnp.einsum(
        "hqk,qhe->khe", probabilities.astype(LOWER), grad_attended, preferred_element_type=WIDE
    )
    grad_probs = jnp.einsum("qhe,khe->hqk", grad_attended, value_heads, preferred_element_type=WIDE)
    grad_scores = (
        probabilities * (grad_probs - jnp.sum(grad_probs * probabilities, axis=-1, keepdims=True))
    ).astype(LOWER)
    grad_query = (
        jnp.einsum("hqk,khe->qhe", grad_scores, key_heads, preferred_element_type=WIDE)
        * score_scale
    )
    grad_key = (
        jnp.einsum("hqk,qhe->khe", grad_scores, query_heads, preferred_element_type=WIDE)
        * score_scale
    )
    return (grad_query, grad_key, grad_value)


def layer_forward(inputs, seq_lengths, matrices, vectors):
    joint_matrix, output_matrix, expand_matrix, reduce_matrix = matrices
    (
        query_bias,
        value_bias,
        output_bias,
        first_gain,
        first_shift,
        expand_bias,
        reduce_bias,
        second_gain,
        second_shift,
    ) = vectors
    row_count, model_width = inputs.shape
    seq_count = seq_lengths.shape[0]
    bias_row = jnp.concatenate([query_bias, jnp.zeros_like(query_bias), value_bias])
    projected = (jnp.dot(inputs, joint_matrix, preferred_element_type=WIDE) + bias_row).astype(
        LOWER
    )
    heads_split = projected.reshape(
        seq_count, row_count // seq_count, 3, HEADS, model_width // HEADS
    )
    query_heads = heads_split[:, :, 0]
    key_heads = heads_split[:, :, 1]
    value_heads = heads_split[:, :, 2]
    attended, log_total = lax.map(attend, (query_heads, key_heads, value_heads, seq_lengths))
    attended = attended.reshape(row_count, model_width).astype(LOWER)
    residual_one = inputs.astype(WIDE) + (
        jnp.dot(attended, output_matrix, preferred_element_type=WIDE) + output_bias
    )
    normal_first, normed_first, inverse_first = norm_forward(residual_one, first_gain, first_shift)
    normal_low = normal_first.astype(LOWER)
    preact = jnp.dot(normal_low, expand_matrix, preferred_element_type=WIDE) + expand_bias
    activation = jax.nn.gelu(preact, approximate=False).astype(LOWER)
    residual_two = normal_first + (
        jnp.dot(activation, reduce_matrix, preferred_element_type=WIDE) + reduce_bias
    )
    output, normed_second, inverse_second = norm_forward(residual_two, second_gain, second_shift)
    stored = (
        inputs,
        query_heads,
        key_heads,
        value_heads,
        seq_lengths,
        log_total,
        attended,
        normed_first,
        inverse_first,
        normal_low,
        preact,
        activation,
        normed_second,
        inverse_second,
    )
    return (output, stored)


def layer_backward(gradient, stored, matrices, vectors):
    (
        inputs,
        query_heads,
        key_heads,
        value_heads,
        seq_lengths,
        log_total,
        attended,
        normed_first,
        inverse_first,
        normal_low,
        preact,
        activation,
        normed_second,
        inverse_second,
    ) = stored
    joint_matrix, output_matrix, expand_matrix, reduce_matrix = matrices
    first_gain = vectors[3]
    second_gain = vectors[7]
    row_count, model_width = inputs.shape
    grad_second = norm_backward(gradient, normed_second, inverse_second, second_gain)
    second_gain_term = jnp.sum(gradient * normed_second, axis=0)
    second_shift_term = jnp.sum(gradient, axis=0)
    grad_branch_two = grad_second.astype(LOWER)
    reduce_bias_term = jnp.sum(grad_branch_two.astype(WIDE), axis=0)
    grad_activation = times_transposed(grad_branch_two, reduce_matrix)
    unused, gelu_back = jax.vjp(partial(jax.nn.gelu, approximate=False), preact)
    grad_preact = gelu_back(grad_activation)[0].astype(LOWER)
    expand_bias_term = jnp.sum(grad_preact.astype(WIDE), axis=0)
    grad_normal = grad_second + times_transposed(grad_preact, expand_matrix)
    grad_first = norm_backward(grad_normal, normed_first, inverse_first, first_gain)
    first_gain_term = jnp.sum(grad_normal * normed_first, axis=0)
    first_shift_term = jnp.sum(grad_normal, axis=0)
    grad_branch_one = grad_first.astype(LOWER)
    output_bias_term = jnp.sum(grad_branch_one.astype(WIDE), axis=0)
    grad_attended = times_transposed(grad_branch_one, output_matrix).astype(LOWER)
    grad_attended = grad_attended.reshape(query_heads.shape)
    grad_query, grad_key, grad_value = lax.map(
        attend_backward,
        (query_heads, key_heads, value_heads, seq_lengths, log_total, grad_attended),
    )
    grad_projected = (
        jnp.stack([grad_query, grad_key, grad_value], axis=2)
        .reshape(row_count, 3 * model_width)
        .astype(LOWER)
    )
    column_sums = jnp.sum(grad_projected.astype(WIDE), axis=0)
    query_bias_term = column_sums[:model_width]
    value_bias_term = column_sums[2 * model_width :]
    grad_inputs = grad_first + times_transposed(grad_projected, joint_matrix)
    product_pairs = (
        (inputs, grad_projected),
        (attended, grad_branch_one),
        (normal_low, grad_preact),
        (activation, grad_branch_two),
    )
    vector_terms = (
        query_bias_term,
        value_bias_term,
        output_bias_term,
        first_gain_term,
        first_shift_term,
        expand_bias_term,
        reduce_bias_term,
        second_gain_term,
        second_shift_term,
    )
    return (grad_inputs, product_pairs, vector_terms)


def scatter_rows(left_rows, right_rows):
    return lax.psum_scatter(
        lax.dot_general(
            left_rows, right_rows, (((0,), (0,)), ((), ())), preferred_element_type=WIDE
        ).astype(jnp.bfloat16),
        "grid",
        scatter_dimension=0,
        tiled=True,
    ).astype(jnp.float32)


def on_device(
    section_edges,
    lengths,
    joint_weight,
    query_bias,
    value_bias,
    output_weight,
    output_bias,
    first_gain,
    first_shift,
    expand_weight,
    expand_bias,
    reduce_weight,
    reduce_bias,
    second_gain,
    second_shift,
):
    first_section = lax.axis_index("section") == 0
    local_edges = section_edges[0]
    micro_count, seq_count, seq_span, model_width = local_edges.shape
    row_count = seq_count * seq_span
    vectors = tuple(
        (
            v[0]
            for v in (
                query_bias,
                value_bias,
                output_bias,
                first_gain,
                first_shift,
                expand_bias,
                reduce_bias,
                second_gain,
                second_shift,
            )
        )
    )
    matrices = (
        lax.all_gather(joint_weight[0], "grid", axis=0, tiled=True),
        lax.all_gather(output_weight[0], "grid", axis=0, tiled=True),
        lax.all_gather(expand_weight[0], "grid", axis=0, tiled=True),
        lax.all_gather(reduce_weight[0], "grid", axis=0, tiled=True),
    )
    received = jnp.zeros((row_count, model_width), LOWER)
    stored_list = []
    outputs = []
    for step_index in range(micro_count + 1):
        own_rows = local_edges[min(step_index, micro_count - 1)].reshape(row_count, model_width)
        inputs = jnp.where(first_section, own_rows, received)
        seq_lengths = jnp.where(
            first_section,
            lengths[min(step_index, micro_count - 1)],
            lengths[max(step_index - 1, 0)],
        )
        output, stored = layer_forward(inputs, seq_lengths, matrices, vectors)
        stored_list.append(stored)
        outputs.append(output)
        if step_index < micro_count:
            received = from_behind(output.astype(LOWER), "section", 1)
    matrices = (
        lax.all_gather(joint_weight[0], "grid", axis=0, tiled=True),
        lax.all_gather(output_weight[0], "grid", axis=0, tiled=True),
        lax.all_gather(expand_weight[0], "grid", axis=0, tiled=True),
        lax.all_gather(reduce_weight[0], "grid", axis=0, tiled=True),
    )
    coming = jnp.zeros((row_count, model_width), LOWER)
    results = []
    vector_total = None
    for step_index in range(micro_count + 1):
        cotangent = (
            local_edges[min(step_index, micro_count - 1)]
            .reshape(row_count, model_width)
            .astype(WIDE)
        )
        gradient = jnp.where(first_section, coming.astype(WIDE), cotangent)
        stored = jax.tree.map(
            lambda first_val, last_val: jnp.where(first_section, first_val, last_val),
            stored_list[max(step_index - 1, 0)],
            stored_list[min(step_index + 1, micro_count)],
        )
        grad_inputs, product_pairs, vector_terms = layer_backward(
            gradient, stored, matrices, vectors
        )
        live_flag = jnp.where(first_section, step_index >= 1, step_index < micro_count).astype(WIDE)
        weighted = tuple((t * live_flag for t in vector_terms))
        vector_total = (
            weighted
            if vector_total is None
            else tuple((a + b for a, b in zip(vector_total, weighted)))
        )
        results.append((grad_inputs, product_pairs))
        if step_index < micro_count:
            coming = from_behind(grad_inputs.astype(LOWER), "section", -1)
    boundary_rows = []
    chosen_pairs = []
    for batch_index in range(micro_count):
        boundary_rows.append(
            jnp.where(first_section, results[batch_index + 1][0], outputs[batch_index + 1])
        )
        chosen_pairs.append(
            jax.tree.map(
                lambda first_val, last_val: jnp.where(first_section, first_val, last_val),
                results[batch_index + 1][1],
                results[batch_index][1],
            )
        )
    boundary = jnp.stack(boundary_rows).reshape(1, micro_count, seq_count, seq_span, model_width)
    factor = 1.0 / math.sqrt(micro_count * row_count * lax.axis_size("dp") * lax.axis_size("grid"))
    left_list = []
    right_list = []
    for pair_index in range(4):
        left_list.append(jnp.concatenate([pairs[pair_index][0] for pairs in chosen_pairs], axis=0))
        right_list.append(jnp.concatenate([pairs[pair_index][1] for pairs in chosen_pairs], axis=0))
    matrix_parts = [scatter_rows(left_list[i], right_list[i]) for i in range(4)]
    summed = (
        lax.psum(matrix_parts[0].astype(jnp.bfloat16), "dp").astype(jnp.float32),
        lax.psum(matrix_parts[1].astype(jnp.bfloat16), "dp").astype(jnp.float32),
        lax.psum(matrix_parts[2].astype(jnp.bfloat16), "dp").astype(jnp.float32),
        lax.psum(matrix_parts[3].astype(jnp.bfloat16), "dp").astype(jnp.float32),
    )
    vector_summed = lax.psum(vector_total, ("dp", "grid"))
    matrix_grads = [(m * factor)[None] for m in summed]
    vector_grads = [(v * factor)[None] for v in vector_summed]
    return (
        boundary,
        matrix_grads[0],
        vector_grads[0],
        vector_grads[1],
        matrix_grads[1],
        vector_grads[2],
        vector_grads[3],
        vector_grads[4],
        matrix_grads[2],
        vector_grads[5],
        matrix_grads[3],
        vector_grads[6],
        vector_grads[7],
        vector_grads[8],
    )


def solution(mesh):
    placed = (
        P("section", None, ("dp", "grid"), None, None),
        P(None, ("dp", "grid")),
        P("section", "grid", None),
        P("section", None),
        P("section", None),
        P("section", "grid", None),
        P("section", None),
        P("section", None),
        P("section", None),
        P("section", "grid", None),
        P("section", None),
        P("section", "grid", None),
        P("section", None),
        P("section", None),
        P("section", None),
    )
    return jax.shard_map(
        on_device,
        mesh=mesh,
        in_specs=placed,
        out_specs=(
            P("section", None, ("dp", "grid"), None, None),
            P("section", "grid", None),
            P("section", None),
            P("section", None),
            P("section", "grid", None),
            P("section", None),
            P("section", None),
            P("section", None),
            P("section", "grid", None),
            P("section", None),
            P("section", "grid", None),
            P("section", None),
            P("section", None),
            P("section", None),
        ),
        check_vma=False,
    )
```

profile of v0, /device:TPU:0, one launch (start us, length us, event | category | flops | bytes accessed | tf_op | source)
XLA Modules:
  0.0 1029.5 jit_solution(7961055840677082789)
XLA Ops:
  17.7 60.4 %all-gather.9.cloned.1.call-done = bf16[1,768,2304]{2,1,0:T(8,128)(2,1)} async-done(((bf16[1,96,2304]{2,1,0:T(8,128)(2,1)}), bf16[1,768,2304]{2,1,0:T(8,128)(2,1)}) %all-gather.9.cloned.1.call-update) | async-done | bytes 3538960 | tf_op jit(solution)/shard_map/all_gather | solution.py:267
  78.1 5.7 fusion.128
  86.6 3.1 fusion
  92.4 4.2 fusion.197
  96.6 23.3 %all-gather.11.cloned.1.call-done = bf16[1,768,768]{2,1,0:T(8,128)(2,1)} async-done(((bf16[1,96,768]{2,1,0:T(8,128)(2,1)}), bf16[1,768,768]{2,1,0:T(8,128)(2,1)}) %all-gather.11.cloned.1.call-update) | async-done | bytes 1179664 | tf_op jit(solution)/shard_map/all_gather | solution.py:268
  122.9 77.9 %all-gather.13.cloned.1.call-done = bf16[1,768,3072]{2,1,0:T(8,128)(2,1)} async-done(((bf16[1,96,3072]{2,1,0:T(8,128)(2,1)}), bf16[1,768,3072]{2,1,0:T(8,128)(2,1)}) %all-gather.13.cloned.1.call-update) | async-done | bytes 4718608 | tf_op jit(solution)/shard_map/all_gather | solution.py:269
  200.8 19.5 %fusion.11 = (bf16[512,3072]{1,0:T(8,128)(2,1)}, f32[512,3072]{1,0:T(8,128)}) fusion(f32[3072]{0:T(1024)S(1)} %bitcast.445, bf16[1,768,3072]{2,1,0:T(8,128)(2,1)} %all-gather.13.cloned.1.call-done, f32[512,768]{1,0:T(8,128)S(1)} %get-tuple-element.293, f32[768]{0:T(1024)S(1)} %reduce.8, f32[768]{0:T(1024)S(1)} %reduce.7, f32[512]{0:T(512)S(1)} %add_rsqrt_fusion.5, ...), kind=kOutput, calls=%fused_computation.35 | convolution fusion | flops 2521694208 | bytes 15751168 | tf_op jit(solution)/shard_map/dot_general | solution.py:122
  220.2 60.6 %all-gather.15.cloned.1.call-done = bf16[1,3072,768]{2,1,0:T(8,128)(2,1)} async-done(((bf16[1,384,768]{2,1,0:T(8,128)(2,1)}), bf16[1,3072,768]{2,1,0:T(8,128)(2,1)}) %all-gather.15.cloned.1.call-update) | async-done | bytes 4718608 | tf_op jit(solution)/shard_map/all_gather | solution.py:270
  280.9 6.1 fusion.285
  298.4 5.7 fusion.129
  304.1 3.0 copy.63
  307.1 3.1 fusion.1
  312.8 4.2 fusion.196
  322.3 19.7 %fusion.14 = (bf16[512,3072]{1,0:T(8,128)(2,1)S(1)}, f32[512,3072]{1,0:T(8,128)}) fusion(f32[3072]{0:T(1024)S(1)} %bitcast.446, bf16[1,768,3072]{2,1,0:T(8,128)(2,1)} %all-gather.13.cloned.1.call-done, f32[512,768]{1,0:T(8,128)S(1)} %get-tuple-element.301, f32[512]{0:T(512)S(1)} %add_rsqrt_fusion.3, f32[512]{0:T(512)S(1)} %broadcast_multiply_fusion.24, ...), kind=kOutput, calls=%fused_computation.38 | convolution fusion | flops 2521694208 | bytes 15751168 | tf_op jit(solution)/shard_map/dot_general | solution.py:122
  349.3 6.4 fusion.235
  357.7 3.4 fusion.130
  364.0 3.1 fusion.2
  370.4 3.3 fusion.195
  378.6 19.9 %select_select_fusion.1 = (bf16[512,3072]{1,0:T(8,128)(2,1)}, bf16[512,3072]{1,0:T(8,128)(2,1)S(1)}, f32[512,3072]{1,0:T(8,128)}) fusion(bf16[512,3072]{1,0:T(8,128)(2,1)S(1)} %copy-done.59, bf16[512,3072]{1,0:T(8,128)(2,1)S(1)} %copy-done.61, pred[]{:T(512)} %eq.3, f32[3072]{0:T(1024)S(1)} %bitcast.447, bf16[512,768]{1,0:T(8,128)(2,1)S(1)} %get-tuple-element.254, ...), kind=kOutput, calls=%fused_computation.220 | convolution fusion | flops 2524446720 | bytes 24391680 | tf_op jit(solution)/shard_map/dot_general | solution.py:122
  403.4 20.5 %convert_reduce_fusion.2 = (f32[3072]{0:T(1024)}, bf16[512,3072]{1,0:T(8,128)(2,1)S(1)}) fusion(bf16[1,3072,768]{2,1,0:T(8,128)(2,1)S(1)} %bitcast.442, f32[512,768]{1,0:T(8,128)S(1)} %get-tuple-element.232, f32[512,3072]{1,0:T(8,128)S(1)} %bitcast.452, f32[512,3072]{1,0:T(8,128)} %get-tuple-element.295, f32[3072]{0:T(1024)S(1)} %bitcast.448, pred[]{:T(512)} %eq.3), kind=kOutput, calls=%fused_computation.67 | convolution fusion | flops 2537419776 | bytes 22044672 | tf_op jit(solution)/shard_map/dot_general | solution.py:41
  424.0 3.8 multiply_reduce_fusion.7
  433.3 11.5 %multiply_reduce_fusion.2 = (f32[12,512]{1,0:T(8,128)S(1)}, f32[12,512,512]{1,2,0:T(8,128)}) fusion(f32[12,512,512]{1,2,0:T(8,128)} %fusion.235, f32[12,512]{1,0:T(8,128)S(1)} %copy-done.82, pred[512]{0:T(512)(128)(4,1)S(1)} %copy-done.129, bf16[512,12,64]{0,2,1:T(8,128)(2,1)S(1)} %bitcast.420, pred[]{:T(512)} %eq.3, ...), kind=kOutput, calls=%fused_computation.7 | convolution fusion | flops 418768896 | bytes 27583488 | tf_op jit(solution)/shard_map/while/body/eval_jaxpr/qhe,khe->hqk/dot_general | solution.py:75
  446.1 7.3 multiply_convert_fusion.2
  458.4 3.9 fusion.164
  466.3 5.4 add_convert_fusion
  474.4 6.4 fusion.236
  483.7 21.2 %convert_reduce_fusion.1 = (f32[3072]{0:T(1024)}, bf16[512,3072]{1,0:T(8,128)(2,1)S(1)}) fusion(f32[512,3072]{1,0:T(8,128)} %get-tuple-element.310, f32[512,3072]{1,0:T(8,128)} %get-tuple-element.295, f32[3072]{0:T(1024)S(1)} %bitcast.449, pred[]{:T(512)} %eq.3, bf16[512,768]{1,0:T(8,128)(2,1)S(1)} %get-tuple-element.234, ...), kind=kOutput, calls=%fused_computation.66 | convolution fusion | flops 2537026560 | bytes 21258240 | tf_op jit(solution)/shard_map/dot_general | solution.py:41
  505.0 3.9 multiply_reduce_fusion.6
  514.4 11.6 %multiply_reduce_fusion.1 = (f32[12,512]{1,0:T(8,128)S(1)}, f32[12,512,512]{1,2,0:T(8,128)}) fusion(f32[12,512,512]{1,2,0:T(8,128)} %fusion.236, f32[12,512]{1,0:T(8,128)S(1)} %copy-done.81, pred[512]{0:T(512)(128)(4,1)S(1)} %copy-done.128, bf16[512,12,64]{0,2,1:T(8,128)(2,1)S(1)} %bitcast.418, pred[]{:T(512)} %eq.3, ...), kind=kOutput, calls=%fused_computation.4 | convolution fusion | flops 418768896 | bytes 27575296 | tf_op jit(solution)/shard_map/while/body/eval_jaxpr/qhe,khe->hqk/dot_general | solution.py:75
  527.4 7.4 multiply_convert_fusion.1
  538.1 3.2 fusion.167
  541.8 6.1 fusion.290
  550.3 6.4 fusion.237
  560.2 22.6 %broadcast_select_fusion.2 = (bf16[512,3072]{1,0:T(8,128)(2,1)}, bf16[512,3072]{1,0:T(8,128)(2,1)}, bf16[512,3072]{1,0:T(8,128)(2,1)S(1)}) fusion(bf16[512,3072]{1,0:T(8,128)(2,1)S(1)} %copy-done.139, bf16[512,3072]{1,0:T(8,128)(2,1)S(1)} %copy-done.137, pred[]{:T(512)} %eq.3, bf16[1,3072,768]{2,1,0:T(8,128)(2,1)} %all-gather.15.cloned.1.call-done, ...), kind=kOutput, calls=%fused_computation.223 | convolution fusion | flops 2537422848 | bytes 34615296 | tf_op jit(solution)/shard_map/dot_general | solution.py:41
  582.9 3.2 multiply_reduce_fusion.5
  591.4 10.2 multiply_reduce_fusion
  601.6 8.6 fusion.170
  612.8 10.6 %multiply_convert_fusion = bf16[12,512,512]{1,2,0:T(8,128)(2,1)S(1)} fusion(f32[12,512,512]{1,2,0:T(8,128)} %get-tuple-element.323, f32[12,512,512]{1,2,0:T(8,128)} %fusion.237, f32[12,512]{1,0:T(8,128)S(1)} %get-tuple-element.322, f32[12,512]{1,0:T(8,128)S(1)} %copy-done.80, pred[512]{0:T(512)(128)(4,1)S(1)} %copy-done.127), kind=kLoop, calls=%fused_computation | loop fusion | flops 18874368 | bytes 31506944 | tf_op jit(solution)/shard_map/while/body/eval_jaxpr/convert_element_type | solution.py:78
  629.4 5.9 convolution_convert_fusion
  635.4 4.4 select_select_fusion
  641.2 7.0 fusion.98
  650.4 9.4 fusion.95
  662.9 75.4 %all-reduce = (f32[768]{0:T(1024)S(1)}, f32[768]{0:T(1024)S(1)}, f32[768]{0:T(1024)S(1)}, f32[768]{0:T(1024)S(1)}, f32[768]{0:T(1024)S(1)}, /*index=5*/f32[3072]...) all-reduce(f32[768]{0:T(1024)S(1)} %add.461, ...), channel_id=1, replica_groups=mesh['dp'=2,'section'=2,'grid'=8] {'dp','grid'}, use_global_device_ids=true, to_apply=%region_38.39 | all-reduce | flops 9216 | bytes 73728 | tf_op jit(solution)/shard_map/psum | solution.py:349
  741.2 17.5 %reduce-scatter.5.cloned.1.call-done = bf16[96,2304]{1,0:T(8,128)(2,1)} async-done(((bf16[768,2304]{1,0:T(8,128)(2,1)}), bf16[96,2304]{1,0:T(8,128)(2,1)}) %reduce-scatter.5.cloned.1.call-update) | async-done | bytes 442384 | tf_op jit(solution)/shard_map/reduce_scatter | solution.py:219
  758.8 98.7 %reduce-scatter.11.cloned.1.call-done = bf16[384,768]{1,0:T(8,128)(2,1)} async-done(((bf16[3072,768]{1,0:T(8,128)(2,1)}), bf16[384,768]{1,0:T(8,128)(2,1)}) %reduce-scatter.11.cloned.1.call-update) | async-done | bytes 589840 | tf_op jit(solution)/shard_map/reduce_scatter | solution.py:219
  857.4 98.8 %reduce-scatter.9.cloned.1.call-done = bf16[96,3072]{1,0:T(8,128)(2,1)} async-done(((bf16[768,3072]{1,0:T(8,128)(2,1)}), bf16[96,3072]{1,0:T(8,128)(2,1)}) %reduce-scatter.9.cloned.1.call-update) | async-done | bytes 589840 | tf_op jit(solution)/shard_map/reduce_scatter | solution.py:219
  958.0 5.6 select_bitcast_fusion
  966.1 48.7 %all-reduce.4.cloned.1.call-done = (bf16[96,2304]{1,0:T(8,128)(2,1)}, bf16[96,768]{1,0:T(8,128)(2,1)}, bf16[96,3072]{1,0:T(8,128)(2,1)}, bf16[384,768]{1,0:T(8,128)(2,1)}) async-done(((bf16[96,2304]{1,0:T(8,128)(2,1)}, bf16[96,768]{1,0:T(8,128)(2,1)}, bf16[96,3072]{1,0:T(8,128)(2,1)}, bf16[384,768]{1,0:T(8,128)(2,1)}), (bf16[96,2304]{1,0:T(8,128)(2,1)}, bf16[96,768]{1,0:T(8,128)(2,1)}, ...) | async-done | bytes 1769488 | tf_op jit(solution)/shard_map/psum | solution.py:344
  (492 shorter events, 131.7 us)
Async XLA Ops:
  7.2 70.9 %all-gather.9.cloned.1.call-start = ((), (), s32[]{:S(2)}) async-start(), calls=%async_computation.8 | async-start | bytes 3981312 | tf_op jit(solution)/shard_map/all_gather | solution.py:267
  7.9 112.0 %all-gather.11.cloned.1.call-start = ((), (), s32[]{:S(2)}) async-start(), calls=%async_computation.9 | async-start | bytes 1327104 | tf_op jit(solution)/shard_map/all_gather | solution.py:268
  8.7 192.1 %all-gather.13.cloned.1.call-start = ((), (), s32[]{:S(2)}) async-start(), calls=%async_computation.10 | async-start | bytes 5308416 | tf_op jit(solution)/shard_map/all_gather | solution.py:269
  9.4 271.4 %all-gather.15.cloned.1.call-start = ((), (), s32[]{:S(2)}) async-start(), calls=%async_computation.11 | async-start | bytes 5308416 | tf_op jit(solution)/shard_map/all_gather | solution.py:270
  10.0 731.3 %reduce-scatter.7.cloned.1.call-start = ((), (), s32[]{:S(2)}) async-start(), calls=%async_computation.5 | async-start | bytes 1327104 | tf_op jit(solution)/shard_map/reduce_scatter | solution.py:219
  15.5 383.0 %copy-start.90 = (f32[768]{0:T(1024)}, f32[768]{0:T(1024)S(1)}, u32[]{:S(2)}) copy-start(f32[768]{0:T(1024)S(1)} %reduce.8) | copy-start | bytes 9220
  17.6 327.5 %copy-start.86 = (f32[768]{0:T(1024)}, f32[768]{0:T(1024)S(1)}, u32[]{:S(2)}) copy-start(f32[768]{0:T(1024)S(1)} %reduce.11) | copy-start | bytes 9220
  96.6 104.2 %copy-start.135 = (f32[1,3072]{1,0:T(1,128)S(1)}, f32[1,3072]{1,0:T(1,128)}, u32[]{:S(2)}) copy-start(f32[1,3072]{1,0:T(1,128)} %param.25) | copy-start | bytes 36868
  122.5 158.3 %copy-start.24 = (f32[512,768]{1,0:T(8,128)}, f32[512,768]{1,0:T(8,128)S(1)}, u32[]{:S(2)}) copy-start(f32[512,768]{1,0:T(8,128)S(1)} %get-tuple-element.293) | copy-start | bytes 4718596
  122.5 382.3 %copy-start.92 = (f32[512]{0:T(512)}, f32[512]{0:T(512)S(1)}, u32[]{:S(2)}) copy-start(f32[512]{0:T(512)S(1)} %broadcast_multiply_fusion.26) | copy-start | bytes 6148
  122.9 97.4 %copy-start.108 = (f32[512]{0:T(512)}, f32[512]{0:T(512)S(1)}, u32[]{:S(2)}) copy-start(f32[512]{0:T(512)S(1)} %multiply_reduce_fusion.19) | copy-start | bytes 6148
  122.9 382.0 %copy-start.100 = (f32[512]{0:T(512)}, f32[512]{0:T(512)S(1)}, u32[]{:S(2)}) copy-start(f32[512]{0:T(512)S(1)} %add_rsqrt_fusion.5) | copy-start | bytes 6148
  287.0 58.1 %copy-start.88 = (f32[512]{0:T(512)}, f32[512]{0:T(512)S(1)}, u32[]{:S(2)}) copy-start(f32[512]{0:T(512)S(1)} %broadcast_multiply_fusion.25) | copy-start | bytes 6148
  288.2 57.0 %copy-start.96 = (f32[512]{0:T(512)}, f32[512]{0:T(512)S(1)}, u32[]{:S(2)}) copy-start(f32[512]{0:T(512)S(1)} %add_rsqrt_fusion.4) | copy-start | bytes 6148
  288.5 9.8 collective-permute-start
  298.4 57.3 %copy-start.39 = (bf16[512,768]{1,0:T(8,128)(2,1)}, bf16[512,768]{1,0:T(8,128)(2,1)S(1)}, u32[]{:S(2)}) copy-start(bf16[512,768]{1,0:T(8,128)(2,1)S(1)} %bitcast_select_fusion.1) | copy-start | bytes 2359300
  307.1 42.2 %copy-start = (bf16[512,2304]{0,1:T(8,128)(2,1)}, bf16[512,2304]{0,1:T(8,128)(2,1)S(1)}, u32[]{:S(2)}) copy-start(bf16[512,2304]{0,1:T(8,128)(2,1)S(1)} %copy.63) | copy-start | bytes 7077892
  319.3 22.7 %slice-start.14 = ((s8[4718592]{0:T(1024)(128)(4,1)}), s8[4194304]{0:T(1024)(128)(4,1)S(1)}, s32[]{:S(2)}) async-start(s8[4718592]{0:T(1024)(128)(4,1)} %bitcast.439), calls=%async_computation.27 | async-start | bytes 8388608
  321.9 102.0 %copy-start.94 = (f32[512]{0:T(512)}, f32[512]{0:T(512)S(1)}, u32[]{:S(2)}) copy-start(f32[512]{0:T(512)S(1)} %broadcast_multiply_fusion.24) | copy-start | bytes 6148
  322.2 101.7 %copy-start.102 = (f32[512]{0:T(512)}, f32[512]{0:T(512)S(1)}, u32[]{:S(2)}) copy-start(f32[512]{0:T(512)S(1)} %add_rsqrt_fusion.3) | copy-start | bytes 6148
  347.8 8.0 collective-permute-start.1
  374.7 23.8 %copy-start.47 = (f32[512,768]{1,0:T(8,128)}, f32[512,768]{1,0:T(8,128)S(1)}, u32[]{:S(2)}) copy-start(f32[512,768]{1,0:T(8,128)S(1)} %get-tuple-element.309) | copy-start | bytes 4718596
  376.4 22.1 %slice-start.16 = ((s8[4718592]{0:T(1024)(128)(4,1)}), s8[4194304]{0:T(1024)(128)(4,1)S(1)}, s32[]{:S(2)}) async-start(s8[4718592]{0:T(1024)(128)(4,1)} %bitcast.441), calls=%async_computation.29 | async-start | bytes 8388608
  376.4 26.9 %slice-start.20 = ((s8[6291456]{0:T(1024)(128)(4,1)}), s8[2097152]{0:T(1024)(128)(4,1)S(1)}, s32[]{:S(2)}) async-start(s8[6291456]{0:T(1024)(128)(4,1)} %bitcast.451), calls=%async_computation.33 | async-start | bytes 4194304
  378.2 20.3 %copy-start.63 = (bf16[512,768]{1,0:T(8,128)(2,1)}, bf16[512,768]{1,0:T(8,128)(2,1)S(1)}, u32[]{:S(2)}) copy-start(bf16[512,768]{1,0:T(8,128)(2,1)S(1)} %get-tuple-element.254) | copy-start | bytes 2359300
  378.6 24.8 %slice-start.21 = ((s8[6291456]{0:T(1024)(128)(4,1)}), s8[4194304]{0:T(1024)(128)(4,1)S(1)}, s32[]{:S(2)}) async-start(s8[6291456]{0:T(1024)(128)(4,1)} %bitcast.451), calls=%async_computation.34 | async-start | bytes 8388608
  401.4 22.6 %slice-start.8 = ((s8[4718592]{0:T(1024)(128)(4,1)}), s8[4194304]{0:T(1024)(128)(4,1)S(1)}, s32[]{:S(2)}) async-start(s8[4718592]{0:T(1024)(128)(4,1)} %bitcast.433), calls=%async_computation.21 | async-start | bytes 8388608
  403.3 20.6 %copy-start.45 = (f32[512,768]{1,0:T(8,128)}, f32[512,768]{1,0:T(8,128)S(1)}, u32[]{:S(2)}) copy-start(f32[512,768]{1,0:T(8,128)S(1)} %get-tuple-element.232) | copy-start | bytes 4718596
  403.4 20.6 %slice-start.9 = ((s8[4718592]{0:T(1024)(128)(4,1)}), s8[524288]{0:T(1024)(128)(4,1)S(1)}, s32[]{:S(2)}) async-start(s8[4718592]{0:T(1024)(128)(4,1)} %bitcast.433), calls=%async_computation.22 | async-start | bytes 1048576
  471.7 9.1 collective-permute-start.2
  480.9 24.0 %slice-start.10 = ((s8[4718592]{0:T(1024)(128)(4,1)}), s8[4194304]{0:T(1024)(128)(4,1)S(1)}, s32[]{:S(2)}) async-start(s8[4718592]{0:T(1024)(128)(4,1)} %bitcast.435), calls=%async_computation.23 | async-start | bytes 8388608
  483.6 21.2 %copy-start.64 = (bf16[512,768]{1,0:T(8,128)(2,1)}, bf16[512,768]{1,0:T(8,128)(2,1)S(1)}, u32[]{:S(2)}) copy-start(bf16[512,768]{1,0:T(8,128)(2,1)S(1)} %get-tuple-element.234) | copy-start | bytes 2359300
  483.6 21.3 %copy-start.26 = (f32[512,768]{1,0:T(8,128)S(1)}, f32[512,768]{1,0:T(8,128)}, u32[]{:S(2)}) copy-start(f32[512,768]{1,0:T(8,128)} %copy-done.24) | copy-start | bytes 4718596
  483.7 21.3 %copy-start.48 = (f32[512,768]{1,0:T(8,128)S(1)}, f32[512,768]{1,0:T(8,128)}, u32[]{:S(2)}) copy-start(f32[512,768]{1,0:T(8,128)} %copy-done.47) | copy-start | bytes 4718596
  483.7 21.3 %slice-start.11 = ((s8[4718592]{0:T(1024)(128)(4,1)}), s8[524288]{0:T(1024)(128)(4,1)S(1)}, s32[]{:S(2)}) async-start(s8[4718592]{0:T(1024)(128)(4,1)} %bitcast.435), calls=%async_computation.24 | async-start | bytes 1048576
  547.9 8.8 collective-permute-start.3
  559.1 23.7 %slice-start.12 = ((s8[4718592]{0:T(1024)(128)(4,1)}), s8[4194304]{0:T(1024)(128)(4,1)S(1)}, s32[]{:S(2)}) async-start(s8[4718592]{0:T(1024)(128)(4,1)} %bitcast.437), calls=%async_computation.25 | async-start | bytes 8388608
  559.6 23.1 %copy-start.51 = (f32[512,768]{1,0:T(8,128)}, f32[512,768]{1,0:T(8,128)S(1)}, u32[]{:S(2)}) copy-start(f32[512,768]{1,0:T(8,128)S(1)} %get-tuple-element.236) | copy-start | bytes 4718596
  560.1 22.6 %copy-start.30 = (f32[512,768]{1,0:T(8,128)S(1)}, f32[512,768]{1,0:T(8,128)}, u32[]{:S(2)}) copy-start(f32[512,768]{1,0:T(8,128)} %copy-done.28) | copy-start | bytes 4718596
  560.2 22.6 %copy-start.49 = (f32[512,768]{1,0:T(8,128)S(1)}, f32[512,768]{1,0:T(8,128)}, u32[]{:S(2)}) copy-start(f32[512,768]{1,0:T(8,128)} %copy-done.47) | copy-start | bytes 4718596
  560.2 22.7 %copy-start.95 = (f32[512]{0:T(512)S(1)}, f32[512]{0:T(512)}, u32[]{:S(2)}) copy-start(f32[512]{0:T(512)} %copy-done.94) | copy-start | bytes 6148
  560.2 22.7 %copy-start.103 = (f32[512]{0:T(512)S(1)}, f32[512]{0:T(512)}, u32[]{:S(2)}) copy-start(f32[512]{0:T(512)} %copy-done.102) | copy-start | bytes 6148
  560.2 22.7 %slice-start.13 = ((s8[4718592]{0:T(1024)(128)(4,1)}), s8[524288]{0:T(1024)(128)(4,1)S(1)}, s32[]{:S(2)}) async-start(s8[4718592]{0:T(1024)(128)(4,1)} %bitcast.437), calls=%async_computation.26 | async-start | bytes 1048576
  612.7 146.0 %reduce-scatter.5.cloned.1.call-start = ((), (), s32[]{:S(2)}) async-start(), calls=%async_computation.4 | async-start | bytes 3981312 | tf_op jit(solution)/shard_map/reduce_scatter | solution.py:219
  635.3 222.1 %reduce-scatter.11.cloned.1.call-start = ((), (), s32[]{:S(2)}) async-start(), calls=%async_computation.7 | async-start | bytes 5308416 | tf_op jit(solution)/shard_map/reduce_scatter | solution.py:219
  648.2 308.0 %reduce-scatter.9.cloned.1.call-start = ((), (), s32[]{:S(2)}) async-start(), calls=%async_computation.6 | async-start | bytes 5308416 | tf_op jit(solution)/shard_map/reduce_scatter | solution.py:219
  659.7 298.3 %copy-start.23 = (f32[512,768]{1,0:T(8,128)S(1)}, f32[512,768]{1,0:T(8,128)}, u32[]{:S(2)}) copy-start(f32[512,768]{1,0:T(8,128)} %copy-done.20) | copy-start | bytes 4718596
  659.8 355.1 %all-reduce.4.cloned.1.call-start = ((), (), s32[]{:S(2)}) async-start(), calls=%async_computation.12 | async-start | bytes 3538944 | tf_op jit(solution)/shard_map/psum | solution.py:344
  (128 other events, 813.4 us)
Sparse Core Ops, SparseCore 0:
  10.2 67.8 all-gather.8
  80.3 39.5 all-gather.10
  122.1 78.6 all-gather.12
  202.8 78.0 all-gather.14
  612.9 63.6 reduce-scatter.6
  680.0 78.6 reduce-scatter.4
  762.4 94.9 reduce-scatter.10
  861.1 95.1 reduce-scatter.8
  958.7 56.0 all-reduce.3
where the time goes:
time: 1040 us; the launch traced here: 1030 us
  waiting for transfers between devices  489 us (47%)
  matrix products  315 us (30%)
  other arithmetic  88.6 us (9%)
  blocking collectives  75.4 us (7%)
  local copies, waits for them, and re-layouts  36.4 us (4%)
  between operations  20.1 us (2%)
    reduce_scatter x4, waiting for transfers between devices, scatter_rows(): lax.psum_scatter(lax.dot_general(left_rows, right_rows, (((0,), (0,)), ((...  215 us
    dot_general x12, matrix products, times_transposed(): lax.dot_general(left_rows, right_rows, (((1,), (1,)), ((), ())), preferre...  97.6 us
    all_gather x1, waiting for transfers between devices, on_device(): lax.all_gather(expand_weight[0], 'grid', axis=0, tiled=True)  77.9 us
    psum x1, blocking collectives, on_device(): vector_summed = lax.psum(vector_total, ('dp', 'grid'))  75.4 us
    all_gather x1, waiting for transfers between devices, on_device(): lax.all_gather(reduce_weight[0], 'grid', axis=0, tiled=True)  60.6 us
    all_gather x1, waiting for transfers between devices, on_device(): lax.all_gather(joint_weight[0], 'grid', axis=0, tiled=True)  60.4 us
    dot_general x3, matrix products, layer_forward(): jnp.dot(normal_low, expand_matrix, preferred_element_type=WIDE)  59.1 us
    psum x1, waiting for transfers between devices, on_device(): lax.psum(matrix_parts[0].astype(jnp.bfloat16), 'dp').astype(jnp.float32)  48.7 us
  transfers between devices with their start and end apart: 13, of which 8 were waited for; matrix products, arithmetic and copies ran while one was open for 13% of the time, Pallas kernels for 0%

commit v1 on v0

v1 whole, which is shorter than its diff:
```python
import math

import jax
import jax.numpy as jnp
from jax import lax
from jax.experimental import pallas as pl
from jax.experimental.pallas import tpu as pltpu
from jax.sharding import PartitionSpec as P

HEADS = 12


EPSILON = 1e-06
MASKED = -1000000000.0
LANES = 128
LOWER = jnp.bfloat16
WIDE = jnp.float32


def norm_forward(residual, gain_vector, shift_vector):
    center = residual - jnp.mean(residual, axis=-1, keepdims=True)
    inverse = lax.rsqrt(jnp.mean(center * center, axis=-1, keepdims=True) + EPSILON)
    normed = center * inverse
    return (normed * gain_vector + shift_vector, normed, inverse)


def norm_backward(gradient, normed, inverse, gain_vector):
    scaled = gradient * gain_vector
    return inverse * (
        scaled
        - jnp.mean(scaled, axis=-1, keepdims=True)
        - normed * jnp.mean(scaled * normed, axis=-1, keepdims=True)
    )


def times_transposed(left_rows, right_rows):
    return lax.dot_general(
        left_rows, right_rows, (((1,), (1,)), ((), ())), preferred_element_type=WIDE
    )


def over_contract(left, right, left_dim, right_dim):
    return lax.dot_general(
        left, right, (((left_dim,), (right_dim,)), ((), ())), preferred_element_type=WIDE
    )


def head_softmax(query, key, length, score_scale):
    scores = over_contract(query, key, 1, 1) * score_scale
    places = lax.broadcasted_iota(jnp.int32, scores.shape, 1)
    scores = jnp.where(places < length, scores, MASKED)
    weights = jnp.exp(scores - jnp.max(scores, axis=-1, keepdims=True))
    return weights * (1.0 / jnp.sum(weights, axis=-1, keepdims=True))


def attend_kernel(head_width, lengths_ref, query_ref, key_ref, value_ref, out_ref):
    length = lengths_ref[pl.program_id(0)]
    query, key, value = query_ref[...], key_ref[...], value_ref[...]
    lane = lax.broadcasted_iota(jnp.int32, query.shape, 1)
    total = jnp.zeros(query.shape, WIDE)
    for part in range(LANES // head_width):
        own = lane // head_width == part
        probs = head_softmax(
            jnp.where(own, query, jnp.zeros_like(query)), key, length, head_width ** (-0.5)
        )
        own_value = jnp.where(own, value, jnp.zeros_like(value))
        total = total + over_contract(probs.astype(LOWER), own_value, 1, 0)
    out_ref[...] = total.astype(LOWER)


def attend_backward_kernel(
    head_width, lengths_ref, query_ref, key_ref, value_ref, grad_ref, out_ref
):
    length = lengths_ref[pl.program_id(0)]
    pair = pl.program_id(1)
    model_width = out_ref.shape[1] // 3
    query, key, value, grad = query_ref[...], key_ref[...], value_ref[...], grad_ref[...]
    lane = lax.broadcasted_iota(jnp.int32, query.shape, 1)
    score_scale = head_width ** (-0.5)
    grad_query = jnp.zeros(query.shape, WIDE)
    grad_key = jnp.zeros(query.shape, WIDE)
    grad_value = jnp.zeros(query.shape, WIDE)
    none = jnp.zeros_like(query)
    for part in range(LANES // head_width):
        own = lane // head_width == part
        own_query = jnp.where(own, query, none)
        own_key = jnp.where(own, key, none)
        own_grad = jnp.where(own, grad, none)
        probs = head_softmax(own_query, key, length, score_scale)
        grad_probs = over_contract(own_grad, value, 1, 1)
        row_term = jnp.sum(grad_probs * probs, axis=-1, keepdims=True)
        grad_scores = (probs * (grad_probs - row_term)).astype(LOWER)
        grad_value = grad_value + over_contract(probs.astype(LOWER), own_grad, 0, 0)
        grad_query = grad_query + over_contract(grad_scores, own_key, 1, 0)
        grad_key = grad_key + over_contract(grad_scores, own_query, 0, 0)
    for place, result in enumerate(
        (grad_query * score_scale, grad_key * score_scale, grad_value)
    ):
        start = pl.multiple_of(place * model_width + pair * LANES, LANES)
        out_ref[:, pl.ds(start, LANES)] = result.astype(LOWER)


def head_blocks(span, first):
    return pl.BlockSpec((span, LANES), lambda s, i: (s, first + i))


def attention(projected, seq_lengths):
    row_count, width = projected.shape
    model_width = width // 3
    seq_count = seq_lengths.shape[0]
    span = row_count // seq_count
    pairs = model_width // LANES
    head_width = model_width // HEADS

    def kernel(*refs):
        attend_kernel(head_width, *refs)

    return pl.pallas_call(
        kernel,
        grid=(seq_count, pairs),
        in_specs=[
            pl.BlockSpec(memory_space=pltpu.SMEM),
            head_blocks(span, 0),
            head_blocks(span, pairs),
            head_blocks(span, 2 * pairs),
        ],
        out_specs=head_blocks(span, 0),
        out_shape=jax.ShapeDtypeStruct((row_count, model_width), LOWER),
        compiler_params=pltpu.CompilerParams(vmem_limit_bytes=32 * 1024 * 1024),
        cost_estimate=pl.CostEstimate(
            flops=8 * row_count * span * model_width,
            bytes_accessed=8 * row_count * model_width,
            transcendentals=row_count * span * HEADS,
        ),
    )(seq_lengths, projected, projected, projected)


def attention_backward(projected, grad_attended, seq_lengths):
    row_count, width = projected.shape
    model_width = width // 3
    seq_count = seq_lengths.shape[0]
    span = row_count // seq_count
    pairs = model_width // LANES
    head_width = model_width // HEADS

    def kernel(*refs):
        attend_backward_kernel(head_width, *refs)

    return pl.pallas_call(
        kernel,
        grid=(seq_count, pairs),
        in_specs=[
            pl.BlockSpec(memory_space=pltpu.SMEM),
            head_blocks(span, 0),
            head_blocks(span, pairs),
            head_blocks(span, 2 * pairs),
            head_blocks(span, 0),
        ],
        out_specs=pl.BlockSpec((span, width), lambda s, i: (s, 0)),
        out_shape=jax.ShapeDtypeStruct((row_count, width), LOWER),
        compiler_params=pltpu.CompilerParams(vmem_limit_bytes=48 * 1024 * 1024),
        cost_estimate=pl.CostEstimate(
            flops=20 * row_count * span * model_width,
            bytes_accessed=14 * row_count * model_width,
            transcendentals=row_count * span * HEADS,
        ),
    )(seq_lengths, projected, projected, projected, grad_attended)


def layer_forward(inputs, seq_lengths, matrices, vectors):
    joint_matrix, output_matrix, expand_matrix, reduce_matrix = matrices
    (
        query_bias,
        value_bias,
        output_bias,
        first_gain,
        first_shift,
        reduce_bias,
        second_gain,
        second_shift,
        expand_bias,
    ) = vectors
    bias_row = jnp.concatenate([query_bias, jnp.zeros_like(query_bias), value_bias])
    projected = (jnp.dot(inputs, joint_matrix, preferred_element_type=WIDE) + bias_row).astype(
        LOWER
    )
    attended = attention(projected, seq_lengths)
    residual_one = inputs.astype(WIDE) + (
        jnp.dot(attended, output_matrix, preferred_element_type=WIDE) + output_bias
    )
    normal_first, normed_first, inverse_first = norm_forward(residual_one, first_gain, first_shift)
    normal_low = normal_first.astype(LOWER)
    preact = jnp.dot(normal_low, expand_matrix, preferred_element_type=WIDE) + expand_bias
    below = 0.5 * (1.0 + lax.erf(preact * math.sqrt(0.5)))
    activation = (preact * below).astype(LOWER)
    slope = below + preact * (jnp.exp(-0.5 * preact * preact) * (1.0 / math.sqrt(2.0 * math.pi)))
    residual_two = normal_first + (
        jnp.dot(activation, reduce_matrix, preferred_element_type=WIDE) + reduce_bias
    )
    output, normed_second, inverse_second = norm_forward(residual_two, second_gain, second_shift)
    stored = (
        inputs,
        projected,
        attended,
        normed_first,
        inverse_first,
        normal_low,
        slope,
        activation,
        normed_second,
        inverse_second,
    )
    return (output, stored)


def layer_backward(gradient, stored, seq_lengths, matrices, vectors):
    (
        inputs,
        projected,
        attended,
        normed_first,
        inverse_first,
        normal_low,
        slope,
        activation,
        normed_second,
        inverse_second,
    ) = stored
    joint_matrix, output_matrix, expand_matrix, reduce_matrix = matrices
    first_gain = vectors[3]
    second_gain = vectors[6]
    model_width = inputs.shape[1]
    grad_second = norm_backward(gradient, normed_second, inverse_second, second_gain)
    second_gain_term = jnp.sum(gradient * normed_second, axis=0)
    second_shift_term = jnp.sum(gradient, axis=0)
    grad_branch_two = grad_second.astype(LOWER)
    reduce_bias_term = jnp.sum(grad_branch_two.astype(WIDE), axis=0)
    grad_preact = (times_transposed(grad_branch_two, reduce_matrix) * slope).astype(LOWER)
    expand_bias_term = jnp.sum(grad_preact.astype(WIDE), axis=0)
    grad_normal = grad_second + times_transposed(grad_preact, expand_matrix)
    grad_first = norm_backward(grad_normal, normed_first, inverse_first, first_gain)
    first_gain_term = jnp.sum(grad_normal * normed_first, axis=0)
    first_shift_term = jnp.sum(grad_normal, axis=0)
    grad_branch_one = grad_first.astype(LOWER)
    output_bias_term = jnp.sum(grad_branch_one.astype(WIDE), axis=0)
    grad_attended = times_transposed(grad_branch_one, output_matrix).astype(LOWER)
    grad_projected = attention_backward(projected, grad_attended, seq_lengths)
    column_sums = jnp.sum(grad_projected.astype(WIDE), axis=0)
    grad_inputs = grad_first + times_transposed(grad_projected, joint_matrix)
    products = tuple(
        over_contract(left, right, 0, 0).astype(LOWER)
        for left, right in (
            (inputs, grad_projected),
            (attended, grad_branch_one),
            (normal_low, grad_preact),
            (activation, grad_branch_two),
        )
    )
    vector_terms = jnp.concatenate(
        [
            column_sums[:model_width],
            column_sums[2 * model_width :],
            output_bias_term,
            first_gain_term,
            first_shift_term,
            reduce_bias_term,
            second_gain_term,
            second_shift_term,
            expand_bias_term,
        ]
    )
    return (grad_inputs, products, vector_terms)


def swap(array, axis, distance=1):
    length = lax.axis_size(axis)
    return lax.ppermute(array, axis, [(i, i ^ distance) for i in range(length)])


def onward(array):
    length = lax.axis_size("grid")
    return lax.ppermute(array, "grid", [(i, (i + 2) % length) for i in range(length)])


def put(buffer, piece, *places):
    starts = tuple(places) + (0,) * (buffer.ndim - len(places))
    shape = (1,) * len(places) + buffer.shape[len(places) :]
    return lax.dynamic_update_slice(buffer, piece.reshape(shape), starts)


def pick(array, place, axis=0):
    return lax.dynamic_index_in_dim(array, place, axis, keepdims=False)


def gather_rows(rows, pair_first):
    size = lax.axis_size("grid")
    steps = size // 2
    here = lax.axis_index("grid")
    column, side = here // 2, here % 2
    buffer = jnp.zeros((steps, 2) + rows.shape, rows.dtype)
    moving = rows
    if pair_first:
        pair = jnp.zeros((2,) + rows.shape, rows.dtype)
        moving = put(put(pair, rows, side), swap(rows, "grid"), 1 - side)
    for step in range(steps):
        place = (column - step) % steps
        if pair_first:
            buffer = put(buffer, moving, place)
        else:
            buffer = put(buffer, moving, place, side)
            buffer = put(buffer, swap(moving, "grid"), place, 1 - side)
        if step < steps - 1:
            moving = onward(moving)
    return buffer.reshape(size * rows.shape[0], rows.shape[1])


def pair_sum(array, side, axis):
    received = swap(pick(array, 1 - side, axis).astype(LOWER), "grid")
    return pick(array, side, axis).astype(WIDE) + received.astype(WIDE)


def ring_sum(array, column):
    steps = array.shape[0]
    moving = pick(array, (column - 1) % steps).astype(WIDE)
    for step in range(steps - 1):
        received = onward(moving.astype(LOWER))
        moving = received.astype(WIDE) + pick(array, (column - 2 - step) % steps).astype(WIDE)
    return moving


def sum_rows(product, pair_last):
    size = lax.axis_size("grid")
    core = lax.axis_index("section")
    here = lax.axis_index("grid")
    column, side = here // 2, here % 2
    rows, width = product.shape
    halves = product.reshape(size // 2, 2, 2, rows // size // 2, width)
    received = swap(pick(halves, 1 - core, 2), "section")
    both = (pick(halves, core, 2).astype(WIDE) + received.astype(WIDE)).astype(LOWER)
    if pair_last:
        total = pair_sum(ring_sum(both, column), side, 0)
    else:
        total = ring_sum(pair_sum(both, side, 1).astype(LOWER), column)
    groups = lax.axis_size("dp")
    sent = total.astype(LOWER)
    for step in range(1, groups):
        received = lax.ppermute(sent, "dp", [(i, (i + step) % groups) for i in range(groups)])
        total = total + received.astype(WIDE)
    return total


def on_device(
    section_edges,
    lengths,
    joint_weight,
    query_bias,
    value_bias,
    output_weight,
    output_bias,
    first_gain,
    first_shift,
    expand_weight,
    expand_bias,
    reduce_weight,
    reduce_bias,
    second_gain,
    second_shift,
):
    core = lax.axis_index("section")
    first_core = core == 0
    edges = section_edges[0]
    micro_count, seq_count, seq_span, model_width = edges.shape
    row_count = seq_count * seq_span
    edges = edges.reshape(micro_count, row_count, model_width)
    kept_edge = pick(edges, core)
    other_edge = swap(pick(edges, 1 - core), "section")
    hidden = jnp.where(first_core, kept_edge, other_edge)
    cotangent = jnp.where(first_core, other_edge, kept_edge)
    seq_lengths = pick(lengths, core)

    def both_layers(own):
        other = swap(own, "section")
        return (jnp.where(first_core, own, other), jnp.where(first_core, other, own))

    vector_list = (
        query_bias,
        value_bias,
        output_bias,
        first_gain,
        first_shift,
        reduce_bias,
        second_gain,
        second_shift,
        expand_bias,
    )
    cuts = []
    for vector in vector_list:
        cuts.append((cuts[-1] if cuts else 0) + vector.shape[1])
    vector_layers = [
        jnp.split(layer, cuts[:-1])
        for layer in both_layers(jnp.concatenate([v[0] for v in vector_list]))
    ]
    matrix_layers = list(
        zip(
            both_layers(gather_rows(joint_weight[0], True)),
            both_layers(gather_rows(output_weight[0], False)),
            both_layers(gather_rows(expand_weight[0], False)),
            both_layers(gather_rows(reduce_weight[0], False)),
        )
    )
    stored_list = []
    for layer in range(2):
        output, stored = layer_forward(
            hidden, seq_lengths, matrix_layers[layer], vector_layers[layer]
        )
        stored_list.append(stored)
        hidden = output.astype(LOWER)
    gradient = cotangent.astype(WIDE)
    sums = [None, None]
    vector_terms = [None, None]
    for layer in (1, 0):
        gradient, products, vector_terms[layer] = layer_backward(
            gradient,
            stored_list[layer],
            seq_lengths,
            matrix_layers[layer],
            vector_layers[layer],
        )
        sums[layer] = [sum_rows(products[i], i == 0) for i in range(4)]
        if layer == 1:
            gradient = gradient.astype(LOWER).astype(WIDE)
    own_rows = jnp.where(first_core, gradient, output)
    other_rows = swap(jnp.where(first_core, output, gradient), "section")
    boundary = put(put(jnp.zeros((2,) + own_rows.shape, WIDE), own_rows, core), other_rows, 1 - core)
    boundary = boundary.reshape(1, micro_count, seq_count, seq_span, model_width)
    positions = lax.axis_size("dp") * lax.axis_size("grid")
    factor = 1.0 / math.sqrt(micro_count * row_count * positions)
    matrix_grads = []
    for index in range(4):
        first_half, second_half = sums[0][index], sums[1][index]
        kept = jnp.where(first_core, first_half, second_half)
        received = swap(jnp.where(first_core, second_half, first_half), "section")
        whole = put(put(jnp.zeros((2,) + kept.shape, WIDE), kept, core), received, 1 - core)
        matrix_grads.append((whole.reshape(-1, kept.shape[-1]) * factor)[None])
    vector_sum = jnp.where(first_core, vector_terms[0], vector_terms[1]) + swap(
        jnp.where(first_core, vector_terms[1], vector_terms[0]), "section"
    )
    for axis in ("dp", "grid"):
        distance = 1
        while distance < lax.axis_size(axis):
            vector_sum = vector_sum + swap(vector_sum, axis, distance)
            distance *= 2
    vector_grads = [part[None] for part in jnp.split(vector_sum * factor, cuts[:-1])]
    return (
        boundary,
        matrix_grads[0],
        vector_grads[0],
        vector_grads[1],
        matrix_grads[1],
        vector_grads[2],
        vector_grads[3],
        vector_grads[4],
        matrix_grads[2],
        vector_grads[8],
        matrix_grads[3],
        vector_grads[5],
        vector_grads[6],
        vector_grads[7],
    )


def solution(mesh):
    placed = (
        P("section", None, ("dp", "grid"), None, None),
        P(None, ("dp", "grid")),
        P("section", "grid", None),
        P("section", None),
        P("section", None),
        P("section", "grid", None),
        P("section", None),
        P("section", None),
        P("section", None),
        P("section", "grid", None),
        P("section", None),
        P("section", "grid", None),
        P("section", None),
        P("section", None),
        P("section", None),
    )
    return jax.shard_map(
        on_device,
        mesh=mesh,
        in_specs=placed,
        out_specs=(
            P("section", None, ("dp", "grid"), None, None),
            P("section", "grid", None),
            P("section", None),
            P("section", None),
            P("section", "grid", None),
            P("section", None),
            P("section", None),
            P("section", None),
            P("section", "grid", None),
            P("section", None),
            P("section", "grid", None),
            P("section", None),
            P("section", None),
            P("section", None),
        ),
        check_vma=False,
    )
```

time: 1040 us -> 672 us (0.65)
  matrix products: 315 us -> 95.3 us
  waiting for transfers between devices: 489 us -> 368 us
  blocking collectives: 75.4 us -> 0 us
  other arithmetic: 88.6 us -> 28 us
  Pallas kernels: 0 us -> 55.8 us
  starting transfers between devices: 5.79 us -> 55.8 us
  local copies, waits for them, and re-layouts: 36.4 us -> 58.7 us
  between operations: 20.1 us -> 3.09 us
    ppermute x4 -> x89, waiting for transfers between devices: 0.01 us -> 368 us  [the longest x36 233 us: onward(): lax.ppermute(array, 'grid', [(i, (i + 2) % length) for i in range(length)])]
    all_gather x4 -> x0, waiting for transfers between devices: 222 us -> none  [the longest x1 77.9 us: on_device(): lax.all_gather(expand_weight[0], 'grid', axis=0, tiled=True)]
    reduce_scatter x4 -> x0, waiting for transfers between devices: 215 us -> none  [scatter_rows(): lax.psum_scatter(lax.dot_general(left_rows, right_rows, (((0,), (0,)), ((...]
    dot_general x25 -> x8, matrix products: 125 us -> 31.2 us  [over_contract(): lax.dot_general(left, right, (((left_dim,), (right_dim,)), ((), ())), pre...]
    psum x1 -> x0, blocking collectives: 75.4 us -> none  [on_device(): vector_summed = lax.psum(vector_total, ('dp', 'grid'))]
    dot_general x12 -> x8, matrix products: 97.6 us -> 32.7 us  [times_transposed(): lax.dot_general(left_rows, right_rows, (((1,), (1,)), ((), ())), preferre...]
    pallas_call x0 -> x4, Pallas kernels: none -> 55.8 us  [the longest x2 34.4 us: attention_backward(): pl.pallas_call(kernel, grid=(seq_count, pairs), in_specs=[pl.BlockSpec(me...]
    ppermute x4 -> x89, starting transfers between devices: 5.43 us -> 55.8 us  [the longest x45 29 us: swap(): return lax.ppermute(array, axis, [(i, i ^ distance) for i in range(length)])]
  transfers between devices with their start and end apart: 13 -> 89, of which waited for: 8 -> 49; matrix products, arithmetic and copies ran while one was open for 13% -> 11% of each run, Pallas kernels for 0% -> 2%
where the time goes in v1:
time: 672 us; the launch traced here: 665 us
  waiting for transfers between devices  368 us (55%)
  matrix products  95.3 us (14%)
  local copies, waits for them, and re-layouts  58.7 us (9%)
  starting transfers between devices  55.8 us (8%)
  Pallas kernels  55.8 us (8%)
  other arithmetic  28 us (4%)
    ppermute x36, waiting for transfers between devices, onward(): lax.ppermute(array, 'grid', [(i, (i + 2) % length) for i in range(length)])  233 us
    ppermute x45, waiting for transfers between devices, swap(): return lax.ppermute(array, axis, [(i, i ^ distance) for i in range(length)])  128 us
    pallas_call x2, Pallas kernels, attention_backward(): pl.pallas_call(kernel, grid=(seq_count, pairs), in_specs=[pl.BlockSpec(me...  34.4 us
    dot_general x8, matrix products, times_transposed(): lax.dot_general(left_rows, right_rows, (((1,), (1,)), ((), ())), preferre...  32.7 us
    dot_general x8, matrix products, over_contract(): lax.dot_general(left, right, (((left_dim,), (right_dim,)), ((), ())), pre...  31.2 us
    ppermute x45, starting transfers between devices, swap(): return lax.ppermute(array, axis, [(i, i ^ distance) for i in range(length)])  29 us
    unnamed x122, local copies, waits for them, and re-layouts  27.8 us
    pallas_call x2, Pallas kernels, attention(): pl.pallas_call(kernel, grid=(seq_count, pairs), in_specs=[pl.BlockSpec(me...  21.3 us
  transfers between devices with their start and end apart: 89, of which 49 were waited for; matrix products, arithmetic and copies ran while one was open for 11% of the time, Pallas kernels for 2%

profile of v1, /device:TPU:0, one launch (start us, length us, event | category | flops | bytes accessed | tf_op | source)
XLA Modules:
  0.0 665.0 jit_solution(11983269403284681397)
XLA Ops:
  35.3 10.4 %collective-permute-done.1 = bf16[96,2304]{1,0:T(8,128)(2,1)S(1)} collective-permute-done((bf16[96,2304]{1,0:T(8,128)(2,1)}, bf16[96,2304]{1,0:T(8,128)(2,1)S(1)}, u32[]{:S(2)}, u32[]{:S(2)}) %collective-permute-start.1) | collective-permute-done | bytes 442400 | tf_op jit(solution)/shard_map/ppermute | solution.py:277
  59.7 6.6 collective-permute-done.17
  68.0 19.0 %collective-permute-done.18 = bf16[96,3072]{1,0:T(8,128)(2,1)S(1)} collective-permute-done((bf16[96,3072]{1,0:T(8,128)(2,1)}, bf16[96,3072]{1,0:T(8,128)(2,1)S(1)}, u32[]{:S(2)}, u32[]{:S(2)}) %collective-permute-start.18) | collective-permute-done | bytes 589856 | tf_op jit(solution)/shard_map/ppermute | solution.py:282
  88.7 11.0 %collective-permute-done.26 = bf16[384,768]{1,0:T(8,128)(2,1)S(1)} collective-permute-done((bf16[384,768]{1,0:T(8,128)(2,1)}, bf16[384,768]{1,0:T(8,128)(2,1)S(1)}, u32[]{:S(2)}, u32[]{:S(2)}) %collective-permute-start.26) | collective-permute-done | bytes 589856 | tf_op jit(solution)/shard_map/ppermute | solution.py:282
  102.3 10.0 %collective-permute-done.20 = bf16[96,3072]{1,0:T(8,128)(2,1)S(1)} collective-permute-done((bf16[96,3072]{1,0:T(8,128)(2,1)S(1)}, bf16[96,3072]{1,0:T(8,128)(2,1)S(1)}, u32[]{:S(2)}, u32[]{:S(2)}) %collective-permute-start.20) | collective-permute-done | bytes 589856 | tf_op jit(solution)/shard_map/ppermute | solution.py:282
  113.8 11.1 %collective-permute-done.28 = bf16[384,768]{1,0:T(8,128)(2,1)S(1)} collective-permute-done((bf16[384,768]{1,0:T(8,128)(2,1)S(1)}, bf16[384,768]{1,0:T(8,128)(2,1)S(1)}, u32[]{:S(2)}, u32[]{:S(2)}) %collective-permute-start.28) | collective-permute-done | bytes 589856 | tf_op jit(solution)/shard_map/ppermute | solution.py:282
  126.5 15.8 %collective-permute-done.3 = bf16[2,96,2304]{2,1,0:T(8,128)(2,1)S(1)} collective-permute-done((bf16[2,96,2304]{2,1,0:T(8,128)(2,1)S(1)}, bf16[2,96,2304]{2,1,0:T(8,128)(2,1)S(1)}, u32[]{:S(2)}, u32[]{:S(2)}) %collective-permute-start.3) | collective-permute-done | bytes 884768 | tf_op jit(solution)/shard_map/ppermute | solution.py:282
  142.4 21.7 %collective-permute-done.4 = bf16[2,96,2304]{2,1,0:T(8,128)(2,1)S(1)} collective-permute-done((bf16[2,96,2304]{2,1,0:T(8,128)(2,1)S(1)}, bf16[2,96,2304]{2,1,0:T(8,128)(2,1)S(1)}, u32[]{:S(2)}, u32[]{:S(2)}) %collective-permute-start.4) | collective-permute-done | bytes 884768 | tf_op jit(solution)/shard_map/ppermute | solution.py:282
  167.6 4.5 collective-permute-done.7
  183.5 4.6 collective-permute-done.13
  190.5 10.8 %shard_map.254 = bf16[512,768]{1,0:T(8,128)(2,1)S(1)} custom-call(s32[1]{0:T(128)} %bitcast.2.refs_0_, bf16[512,2304]{1,0:T(8,128)(2,1)S(1)} %fusion.16.refs_1_.refs_2_.refs_3_, bf16[512,2304]{1,0:T(8,128)(2,1)S(1)} %fusion.16.refs_1_.refs_2_.refs_3_, bf16[512,2304]{1,0:T(8,128)(2,1)S(1)} %fusion.16.refs_1_.refs_2_.refs_3_), custom_call_target="tpu_custom_call" | custom-call | flops 1610612736 | bytes 3145728 | tf_op jit(solution)/shard_map/pallas_call | solution.py:118
  202.5 5.8 multiply_convert_fusion.1
  208.3 4.9 fusion.103
  217.9 10.6 %shard_map.255 = bf16[512,768]{1,0:T(8,128)(2,1)S(1)} custom-call(s32[1]{0:T(128)} %bitcast.2.refs_0_, bf16[512,2304]{1,0:T(8,128)(2,1)S(1)} %fusion.17.refs_1_.refs_2_.refs_3_, bf16[512,2304]{1,0:T(8,128)(2,1)S(1)} %fusion.17.refs_1_.refs_2_.refs_3_, bf16[512,2304]{1,0:T(8,128)(2,1)S(1)} %fusion.17.refs_1_.refs_2_.refs_3_), custom_call_target="tpu_custom_call" | custom-call | flops 1610612736 | bytes 3145728 | tf_op jit(solution)/shard_map/pallas_call | solution.py:118
  230.8 6.1 multiply_convert_fusion
  236.9 6.3 fusion.105
  250.6 8.7 %convert_reduce_fusion = (f32[3072]{0:T(1024)S(1)}, bf16[512,3072]{1,0:T(8,128)(2,1)}) fusion(f32[512,3072]{1,0:T(8,128)} %get-tuple-element.82, f32[3072]{0:T(1024)S(1)} %split.122, bf16[3072,768]{1,0:T(8,128)(2,1)} %collective-permute-done.30, bf16[3072,768]{1,0:T(8,128)(2,1)S(1)} %bitcast.358, pred[]{:T(512)S(6)} %eq.64, ...), kind=kOutput, calls=%fused_computation.14 | convolution fusion | flops 2439115776 | bytes 20471808 | tf_op jit(solution)/shard_map/dot_general | solution.py:37
  259.3 7.0 %convolution_convert_fusion.2 = bf16[768,3072]{1,0:T(8,128)(2,1)} fusion(bf16[512,3072]{1,0:T(8,128)(2,1)} %get-tuple-element.91, f32[512,768]{1,0:T(8,128)S(1)} %get-tuple-element.80, f32[768]{0:T(1024)S(1)} %get-tuple-element.58, f32[768]{0:T(1024)S(1)} %get-tuple-element.59, f32[512]{0:T(512)S(1)} %add_rsqrt_fusion.1, f32[512]{0:T(512)S(1)} %broadcast_multiply_fusion.13), kind=kOutput, calls=%fused_computation.22 | convolution fusion | flops 2420244480 | bytes 9447424 | tf_op jit(solution)/shard_map/dot_general | solution.py:43
  266.3 5.5 multiply_reduce_fusion
  275.0 17.0 %shard_map.256 = bf16[512,2304]{1,0:T(8,128)(2,1)S(1)} custom-call(s32[1]{0:T(128)} %bitcast.2.refs_0_, bf16[512,2304]{1,0:T(8,128)(2,1)S(1)} %fusion.17.refs_1_.refs_2_.refs_3_, bf16[512,2304]{1,0:T(8,128)(2,1)S(1)} %fusion.17.refs_1_.refs_2_.refs_3_, bf16[512,2304]{1,0:T(8,128)(2,1)S(1)} %fusion.17.refs_1_.refs_2_.refs_3_, ...), custom_call_target="tpu_custom_call" | custom-call | flops 4026531840 | bytes 5505024 | tf_op jit(solution)/shard_map/pallas_call | solution.py:149
  300.7 4.5 convolution_convert_fusion.1
  305.3 6.8 %convert_reduce_fusion.1 = (f32[3072]{0:T(1024)S(1)}, bf16[512,3072]{1,0:T(8,128)(2,1)S(1)}) fusion(f32[512,3072]{1,0:T(8,128)} %get-tuple-element.76, f32[3072]{0:T(1024)S(1)} %split.113, bf16[3072,768]{1,0:T(8,128)(2,1)S(1)} %bitcast.361, bf16[3072,768]{1,0:T(8,128)(2,1)} %collective-permute-done.30, pred[]{:T(512)S(6)} %eq.64, ...), kind=kOutput, calls=%fused_computation.15 | convolution fusion | flops 2439115776 | bytes 20471808 | tf_op jit(solution)/shard_map/dot_general | solution.py:37
  313.8 4.9 convolution_convert_fusion.3
  318.7 5.1 multiply_reduce_fusion.1
  325.1 17.4 %shard_map.257 = bf16[512,2304]{1,0:T(8,128)(2,1)S(1)} custom-call(s32[1]{0:T(128)} %bitcast.2.refs_0_, bf16[512,2304]{1,0:T(8,128)(2,1)S(1)} %fusion.16.refs_1_.refs_2_.refs_3_, bf16[512,2304]{1,0:T(8,128)(2,1)S(1)} %fusion.16.refs_1_.refs_2_.refs_3_, bf16[512,2304]{1,0:T(8,128)(2,1)S(1)} %fusion.16.refs_1_.refs_2_.refs_3_, ...), custom_call_target="tpu_custom_call" | custom-call | flops 4026531840 | bytes 5505024 | tf_op jit(solution)/shard_map/pallas_call | solution.py:149
  373.7 4.6 collective-permute-done.49
  382.0 7.5 %collective-permute-done.57 = bf16[4,48,768]{2,1,0:T(8,128)(2,1)S(1)} collective-permute-done((bf16[4,48,768]{2,1,0:T(8,128)(2,1)S(1)}, bf16[4,48,768]{2,1,0:T(8,128)(2,1)S(1)}, u32[]{:S(2)}, u32[]{:S(2)}) %collective-permute-start.57) | collective-permute-done | bytes 294944 | tf_op jit(solution)/shard_map/ppermute | solution.py:277
  389.7 5.8 collective-permute-done.51
  396.2 5.8 collective-permute-done.52
  403.0 5.3 collective-permute-done.53
  431.3 13.4 %collective-permute-done.39 = bf16[2,48,2304]{2,1,0:T(8,128)(2,1)S(1)} collective-permute-done((bf16[2,48,2304]{2,1,0:T(8,128)(2,1)S(1)}, bf16[2,48,2304]{2,1,0:T(8,128)(2,1)S(1)}, u32[]{:S(2)}, u32[]{:S(2)}) %collective-permute-start.39) | collective-permute-done | bytes 442400 | tf_op jit(solution)/shard_map/ppermute | solution.py:282
  444.9 13.0 %collective-permute-done.33 = bf16[2,48,2304]{2,1,0:T(8,128)(2,1)S(1)} collective-permute-done((bf16[2,48,2304]{2,1,0:T(8,128)(2,1)S(1)}, bf16[2,48,2304]{2,1,0:T(8,128)(2,1)S(1)}, u32[]{:S(2)}, u32[]{:S(2)}) %collective-permute-start.33) | collective-permute-done | bytes 442400 | tf_op jit(solution)/shard_map/ppermute | solution.py:282
  466.4 6.7 %collective-permute-done.40 = bf16[2,48,2304]{2,1,0:T(8,128)(2,1)S(1)} collective-permute-done((bf16[2,48,2304]{2,1,0:T(8,128)(2,1)S(1)}, bf16[2,48,2304]{2,1,0:T(8,128)(2,1)S(1)}, u32[]{:S(2)}, u32[]{:S(2)}) %collective-permute-start.40) | collective-permute-done | bytes 442400 | tf_op jit(solution)/shard_map/ppermute | solution.py:282
  473.7 6.2 collective-permute-done.34
  480.0 11.2 %collective-permute-done.41 = bf16[2,48,2304]{2,1,0:T(8,128)(2,1)S(1)} collective-permute-done((bf16[2,48,2304]{2,1,0:T(8,128)(2,1)S(1)}, bf16[2,48,2304]{2,1,0:T(8,128)(2,1)S(1)}, u32[]{:S(2)}, u32[]{:S(2)}) %collective-permute-start.41) | collective-permute-done | bytes 442400 | tf_op jit(solution)/shard_map/ppermute | solution.py:282
  491.4 10.2 %collective-permute-done.35 = bf16[2,48,2304]{2,1,0:T(8,128)(2,1)S(1)} collective-permute-done((bf16[2,48,2304]{2,1,0:T(8,128)(2,1)S(1)}, bf16[2,48,2304]{2,1,0:T(8,128)(2,1)S(1)}, u32[]{:S(2)}, u32[]{:S(2)}) %collective-permute-start.35) | collective-permute-done | bytes 442400 | tf_op jit(solution)/shard_map/ppermute | solution.py:282
  502.3 65.4 %collective-permute-done.42 = bf16[48,2304]{1,0:T(8,128)(2,1)S(1)} collective-permute-done((bf16[48,2304]{1,0:T(8,128)(2,1)S(1)}, bf16[48,2304]{1,0:T(8,128)(2,1)S(1)}, u32[]{:S(2)}, u32[]{:S(2)}) %collective-permute-start.42) | collective-permute-done | bytes 221216 | tf_op jit(solution)/shard_map/ppermute | solution.py:277
  568.2 5.4 collective-permute-done.36
  583.0 4.9 collective-permute-done.84
  588.6 5.6 collective-permute-done.78
  594.9 5.6 collective-permute-done.71
  601.2 5.7 collective-permute-done.65
  607.6 5.6 collective-permute-done.85
  613.9 5.6 collective-permute-done.79
  620.2 5.6 collective-permute-done.72
  626.5 5.7 collective-permute-done.66
  632.8 5.7 collective-permute-done.86
  639.1 5.6 collective-permute-done.80
  (478 shorter events, 209.8 us)
Async XLA Ops:
  0.7 49.0 %collective-permute-start.15 = (bf16[96,3072]{1,0:T(8,128)(2,1)}, bf16[96,3072]{1,0:T(8,128)(2,1)}, u32[]{:S(2)}, u32[]{:S(2)}) collective-permute-start(bf16[96,3072]{1,0:T(8,128)(2,1)} %bitcast.374), channel_id=1, source_target_pairs={{0,1},{1,0},{2,3},{3,2},{4,5},{5,4},{6,7},{7,6},{8,9},{9,8},{10,11... | collective-permute-start | bytes 1769480 | tf_op jit(solution)/shard_map/ppermute | solution.py:277
  3.7 46.1 %collective-permute-start.16 = (bf16[96,3072]{1,0:T(8,128)(2,1)}, bf16[96,3072]{1,0:T(8,128)(2,1)}, u32[]{:S(2)}, u32[]{:S(2)}) collective-permute-start(bf16[96,3072]{1,0:T(8,128)(2,1)} %bitcast.375), channel_id=1, source_target_pairs={{0,2},{1,3},{2,4},{3,5},{4,6},{5,7},{6,0},{7,1},{8,10},{9,11},{10,... | collective-permute-start | bytes 1769480 | tf_op jit(solution)/shard_map/ppermute | solution.py:282
  5.3 47.4 %collective-permute-start.23 = (bf16[384,768]{1,0:T(8,128)(2,1)}, bf16[384,768]{1,0:T(8,128)(2,1)}, u32[]{:S(2)}, u32[]{:S(2)}) collective-permute-start(bf16[384,768]{1,0:T(8,128)(2,1)} %bitcast.376), channel_id=1, source_target_pairs={{0,1},{1,0},{2,3},{3,2},{4,5},{5,4},{6,7},{7,6},{8,9},{9,8},{10,11... | collective-permute-start | bytes 1769480 | tf_op jit(solution)/shard_map/ppermute | solution.py:277
  5.8 48.5 %collective-permute-start.24 = (bf16[384,768]{1,0:T(8,128)(2,1)}, bf16[384,768]{1,0:T(8,128)(2,1)}, u32[]{:S(2)}, u32[]{:S(2)}) collective-permute-start(bf16[384,768]{1,0:T(8,128)(2,1)} %bitcast.377), channel_id=1, source_target_pairs={{0,2},{1,3},{2,4},{3,5},{4,6},{5,7},{6,0},{7,1},{8,10},{9,11},{10,... | collective-permute-start | bytes 1769480 | tf_op jit(solution)/shard_map/ppermute | solution.py:282
  45.7 119.3 %collective-permute-start.8 = (bf16[96,768]{1,0:T(8,128)(2,1)}, bf16[96,768]{1,0:T(8,128)(2,1)S(1)}, u32[]{:S(2)}, u32[]{:S(2)}) collective-permute-start(bf16[96,768]{1,0:T(8,128)(2,1)} %bitcast.380), channel_id=1, source_target_pairs={{0,2},{1,3},{2,4},{3,5},{4,6},{5,7},{6,0},{7,1},{8,10},{9,11},{10,... | collective-permute-start | bytes 442376 | tf_op jit(solution)/shard_map/ppermute | solution.py:282
  49.7 50.9 %collective-permute-start.2 = (bf16[2,96,2304]{2,1,0:T(8,128)(2,1)}, bf16[2,96,2304]{2,1,0:T(8,128)(2,1)S(1)}, u32[]{:S(2)}, u32[]{:S(2)}) collective-permute-start(bf16[2,96,2304]{2,1,0:T(8,128)(2,1)} %bitcast_dynamic-update-slice_fusion.28), channel_id=1, source_target_pairs={{0,2},{1,3},{2,4},{3,5},{4,6},{5,7},{6,0},{7,1},{8,10},{9,11},{10,... | collective-permute-start | bytes 2654216 | tf_op jit(solution)/shard_map/ppermute | solution.py:282
  49.8 16.5 %collective-permute-start.17 = (bf16[96,3072]{1,0:T(8,128)(2,1)}, bf16[96,3072]{1,0:T(8,128)(2,1)S(1)}, u32[]{:S(2)}, u32[]{:S(2)}) collective-permute-start(bf16[96,3072]{1,0:T(8,128)(2,1)} %collective-permute-done.16), channel_id=1, source_target_pairs={{0,1},{1,0},{2,3},{3,2},{4,5},{5,4},{6,7},{7,6},{8,9},{9,8},{10,11... | collective-permute-start | bytes 1769480 | tf_op jit(solution)/shard_map/ppermute | solution.py:277
  52.6 34.4 %collective-permute-start.18 = (bf16[96,3072]{1,0:T(8,128)(2,1)}, bf16[96,3072]{1,0:T(8,128)(2,1)S(1)}, u32[]{:S(2)}, u32[]{:S(2)}) collective-permute-start(bf16[96,3072]{1,0:T(8,128)(2,1)} %collective-permute-done.16), channel_id=1, source_target_pairs={{0,2},{1,3},{2,4},{3,5},{4,6},{5,7},{6,0},{7,1},{8,10},{9,11},{10,... | collective-permute-start | bytes 1769480 | tf_op jit(solution)/shard_map/ppermute | solution.py:282
  54.3 34.3 %collective-permute-start.25 = (bf16[384,768]{1,0:T(8,128)(2,1)}, bf16[384,768]{1,0:T(8,128)(2,1)S(1)}, u32[]{:S(2)}, u32[]{:S(2)}) collective-permute-start(bf16[384,768]{1,0:T(8,128)(2,1)} %collective-permute-done.24), channel_id=1, source_target_pairs={{0,1},{1,0},{2,3},{3,2},{4,5},{5,4},{6,7},{7,6},{8,9},{9,8},{10,11... | collective-permute-start | bytes 1769480 | tf_op jit(solution)/shard_map/ppermute | solution.py:277
  66.3 33.3 %collective-permute-start.26 = (bf16[384,768]{1,0:T(8,128)(2,1)}, bf16[384,768]{1,0:T(8,128)(2,1)S(1)}, u32[]{:S(2)}, u32[]{:S(2)}) collective-permute-start(bf16[384,768]{1,0:T(8,128)(2,1)} %collective-permute-done.24), channel_id=1, source_target_pairs={{0,2},{1,3},{2,4},{3,5},{4,6},{5,7},{6,0},{7,1},{8,10},{9,11},{10,... | collective-permute-start | bytes 1769480 | tf_op jit(solution)/shard_map/ppermute | solution.py:282
  88.6 23.7 %collective-permute-start.20 = (bf16[96,3072]{1,0:T(8,128)(2,1)S(1)}, bf16[96,3072]{1,0:T(8,128)(2,1)S(1)}, u32[]{:S(2)}, u32[]{:S(2)}) collective-permute-start(bf16[96,3072]{1,0:T(8,128)(2,1)S(1)} %collective-permute-done.18), channel_id=1, source_target_pairs={{0,2},{1,3},{2,4},{3,5},{4,6},{5,7},{6,0},{7,1},{8,10},{9,11},{10,... | collective-permute-start | bytes 1769480 | tf_op jit(solution)/shard_map/ppermute | solution.py:282
  99.6 25.3 %collective-permute-start.28 = (bf16[384,768]{1,0:T(8,128)(2,1)S(1)}, bf16[384,768]{1,0:T(8,128)(2,1)S(1)}, u32[]{:S(2)}, u32[]{:S(2)}) collective-permute-start(bf16[384,768]{1,0:T(8,128)(2,1)S(1)} %collective-permute-done.26), channel_id=1, source_target_pairs={{0,2},{1,3},{2,4},{3,5},{4,6},{5,7},{6,0},{7,1},{8,10},{9,11},{10,... | collective-permute-start | bytes 1769480 | tf_op jit(solution)/shard_map/ppermute | solution.py:282
  100.6 41.7 %collective-permute-start.3 = (bf16[2,96,2304]{2,1,0:T(8,128)(2,1)S(1)}, bf16[2,96,2304]{2,1,0:T(8,128)(2,1)S(1)}, u32[]{:S(2)}, u32[]{:S(2)}) collective-permute-start(bf16[2,96,2304]{2,1,0:T(8,128)(2,1)S(1)} %collective-permute-done.2), channel_id=1, source_target_pairs={{0,2},{1,3},{2,4},{3,5},{4,6},{5,7},{6,0},{7,1},{8,10},{9,11},{10,... | collective-permute-start | bytes 2654216 | tf_op jit(solution)/shard_map/ppermute | solution.py:282
  100.7 66.1 %collective-permute-start.27 = (bf16[384,768]{1,0:T(8,128)(2,1)S(1)}, bf16[384,768]{1,0:T(8,128)(2,1)S(1)}, u32[]{:S(2)}, u32[]{:S(2)}) collective-permute-start(bf16[384,768]{1,0:T(8,128)(2,1)S(1)} %collective-permute-done.26), channel_id=1, source_target_pairs={{0,1},{1,0},{2,3},{3,2},{4,5},{5,4},{6,7},{7,6},{8,9},{9,8},{10,11... | collective-permute-start | bytes 1769480 | tf_op jit(solution)/shard_map/ppermute | solution.py:277
  112.3 52.1 %collective-permute-start.21 = (bf16[96,3072]{1,0:T(8,128)(2,1)S(1)}, bf16[96,3072]{1,0:T(8,128)(2,1)S(1)}, u32[]{:S(2)}, u32[]{:S(2)}) collective-permute-start(bf16[96,3072]{1,0:T(8,128)(2,1)S(1)} %collective-permute-done.20), channel_id=1, source_target_pairs={{0,1},{1,0},{2,3},{3,2},{4,5},{5,4},{6,7},{7,6},{8,9},{9,8},{10,11... | collective-permute-start | bytes 1769480 | tf_op jit(solution)/shard_map/ppermute | solution.py:277
  124.9 42.6 %collective-permute-start.29 = (bf16[384,768]{1,0:T(8,128)(2,1)S(1)}, bf16[384,768]{1,0:T(8,128)(2,1)S(1)}, u32[]{:S(2)}, u32[]{:S(2)}) collective-permute-start(bf16[384,768]{1,0:T(8,128)(2,1)S(1)} %collective-permute-done.28), channel_id=1, source_target_pairs={{0,1},{1,0},{2,3},{3,2},{4,5},{5,4},{6,7},{7,6},{8,9},{9,8},{10,11... | collective-permute-start | bytes 1769480 | tf_op jit(solution)/shard_map/ppermute | solution.py:277
  142.3 21.9 %collective-permute-start.4 = (bf16[2,96,2304]{2,1,0:T(8,128)(2,1)S(1)}, bf16[2,96,2304]{2,1,0:T(8,128)(2,1)S(1)}, u32[]{:S(2)}, u32[]{:S(2)}) collective-permute-start(bf16[2,96,2304]{2,1,0:T(8,128)(2,1)S(1)} %collective-permute-done.3), channel_id=1, source_target_pairs={{0,2},{1,3},{2,4},{3,5},{4,6},{5,7},{6,0},{7,1},{8,10},{9,11},{10,... | collective-permute-start | bytes 2654216 | tf_op jit(solution)/shard_map/ppermute | solution.py:282
  164.3 24.1 %collective-permute-start.5 = (bf16[768,2304]{1,0:T(8,128)(2,1)S(1)}, bf16[768,2304]{1,0:T(8,128)(2,1)S(1)}, u32[]{:S(2)}, u32[]{:S(2)}) collective-permute-start(bf16[768,2304]{1,0:T(8,128)(2,1)S(1)} %bitcast.366), channel_id=1, source_target_pairs={{0,8},{8,0},{1,9},{9,1},{2,10},{10,2},{3,11},{11,3},{4,12},{12,4},... | collective-permute-start | bytes 10616840 | tf_op jit(solution)/shard_map/ppermute | solution.py:277
  164.4 38.1 %collective-permute-start.22 = (bf16[768,3072]{1,0:T(8,128)(2,1)S(1)}, bf16[768,3072]{1,0:T(8,128)(2,1)S(1)}, u32[]{:S(2)}, u32[]{:S(2)}) collective-permute-start(bf16[768,3072]{1,0:T(8,128)(2,1)S(1)} %bitcast.348), channel_id=1, source_target_pairs={{0,8},{8,0},{1,9},{9,1},{2,10},{10,2},{3,11},{11,3},{4,12},{12,4},... | collective-permute-start | bytes 14155784 | tf_op jit(solution)/shard_map/ppermute | solution.py:277
  172.1 36.2 %collective-permute-start.30 = (bf16[3072,768]{1,0:T(8,128)(2,1)S(1)}, bf16[3072,768]{1,0:T(8,128)(2,1)}, u32[]{:S(2)}, u32[]{:S(2)}) collective-permute-start(bf16[3072,768]{1,0:T(8,128)(2,1)S(1)} %bitcast.355), channel_id=1, source_target_pairs={{0,8},{8,0},{1,9},{9,1},{2,10},{10,2},{3,11},{11,3},{4,12},{12,4},... | collective-permute-start | bytes 14155784 | tf_op jit(solution)/shard_map/ppermute | solution.py:277
  349.5 108.8 %collective-permute-start.82 = (bf16[4,2,192,768]{3,2,0,1:T(8,128)(2,1)}, bf16[4,2,192,768]{3,2,0,1:T(8,128)(2,1)}, u32[]{:S(2)}, u32[]{:S(2)}) collective-permute-start(bf16[4,2,192,768]{3,2,0,1:T(8,128)(2,1)} %bitcast.323), channel_id=1, source_target_pairs={{0,8},{8,0},{1,9},{9,1},{2,10},{10,2},{3,11},{11,3},{4,12},{12,4},... | collective-permute-start | bytes 7077896 | tf_op jit(solution)/shard_map/ppermute | solution.py:277
  354.9 23.4 %collective-permute-start.56 = (bf16[4,2,48,768]{3,2,0,1:T(8,128)(2,1)}, bf16[4,2,48,768]{3,2,0,1:T(8,128)(2,1)}, u32[]{:S(2)}, u32[]{:S(2)}) collective-permute-start(bf16[4,2,48,768]{3,2,0,1:T(8,128)(2,1)} %bitcast.325), channel_id=1, source_target_pairs={{0,8},{8,0},{1,9},{9,1},{2,10},{10,2},{3,11},{11,3},{4,12},{12,4},... | collective-permute-start | bytes 1769480 | tf_op jit(solution)/shard_map/ppermute | solution.py:277
  373.6 53.5 %collective-permute-start.38 = (bf16[4,2,48,2304]{3,2,1,0:T(8,128)(2,1)S(1)}, bf16[4,2,48,2304]{3,2,1,0:T(8,128)(2,1)S(1)}, u32[]{:S(2)}, u32[]{:S(2)}) collective-permute-start(bf16[4,2,48,2304]{3,2,1,0:T(8,128)(2,1)S(1)} %dynamic-slice_bitcast_fusion.2), channel_id=1, source_target_pairs={{0,8},{8,0},{1,9},{9,1},{2,10},{10,2},{3,11},{11,3},{4,12},{12,4},... | collective-permute-start | bytes 5308424 | tf_op jit(solution)/shard_map/ppermute | solution.py:277
  378.3 48.5 %collective-permute-start.31 = (f32[512,768]{1,0:T(8,128)S(1)}, f32[512,768]{1,0:T(8,128)S(1)}, u32[]{:S(2)}, u32[]{:S(2)}) collective-permute-start(f32[512,768]{1,0:T(8,128)S(1)} %fusion.48), channel_id=1, source_target_pairs={{0,8},{8,0},{1,9},{9,1},{2,10},{10,2},{3,11},{11,3},{4,12},{12,4},... | collective-permute-start | bytes 4718600 | tf_op jit(solution)/shard_map/ppermute | solution.py:277
  380.4 15.0 %collective-permute-start.51 = (bf16[4,48,768]{2,1,0:T(8,128)(2,1)S(1)}, bf16[4,48,768]{2,1,0:T(8,128)(2,1)S(1)}, u32[]{:S(2)}, u32[]{:S(2)}) collective-permute-start(bf16[4,48,768]{2,1,0:T(8,128)(2,1)S(1)} %dynamic-slice_bitcast_fusion.17), channel_id=1, source_target_pairs={{0,1},{1,0},{2,3},{3,2},{4,5},{5,4},{6,7},{7,6},{8,9},{9,8},{10,11... | collective-permute-start | bytes 884744 | tf_op jit(solution)/shard_map/ppermute | solution.py:277
  421.4 39.4 %collective-permute-start.76 = (bf16[4,2,192,768]{3,2,1,0:T(8,128)(2,1)}, bf16[4,2,192,768]{3,2,1,0:T(8,128)(2,1)S(1)}, u32[]{:S(2)}, u32[]{:S(2)}) collective-permute-start(bf16[4,2,192,768]{3,2,1,0:T(8,128)(2,1)} %dynamic-slice_bitcast_fusion), channel_id=1, source_target_pairs={{0,8},{8,0},{1,9},{9,1},{2,10},{10,2},{3,11},{11,3},{4,12},{12,4},... | collective-permute-start | bytes 7077896 | tf_op jit(solution)/shard_map/ppermute | solution.py:277
  426.9 35.2 %collective-permute-start.69 = (bf16[4,2,48,3072]{3,2,0,1:T(8,128)(2,1)}, bf16[4,2,48,3072]{3,2,0,1:T(8,128)(2,1)S(1)}, u32[]{:S(2)}, u32[]{:S(2)}) collective-permute-start(bf16[4,2,48,3072]{3,2,0,1:T(8,128)(2,1)} %bitcast.324), channel_id=1, source_target_pairs={{0,8},{8,0},{1,9},{9,1},{2,10},{10,2},{3,11},{11,3},{4,12},{12,4},... | collective-permute-start | bytes 7077896 | tf_op jit(solution)/shard_map/ppermute | solution.py:277
  429.8 34.9 %collective-permute-start.63 = (bf16[4,2,48,3072]{3,2,1,0:T(8,128)(2,1)S(1)}, bf16[4,2,48,3072]{3,2,1,0:T(8,128)(2,1)S(1)}, u32[]{:S(2)}, u32[]{:S(2)}) collective-permute-start(bf16[4,2,48,3072]{3,2,1,0:T(8,128)(2,1)S(1)} %copy-done.18), channel_id=1, source_target_pairs={{0,8},{8,0},{1,9},{9,1},{2,10},{10,2},{3,11},{11,3},{4,12},{12,4},... | collective-permute-start | bytes 7077896 | tf_op jit(solution)/shard_map/ppermute | solution.py:277
  458.0 15.1 %collective-permute-start.40 = (bf16[2,48,2304]{2,1,0:T(8,128)(2,1)S(1)}, bf16[2,48,2304]{2,1,0:T(8,128)(2,1)S(1)}, u32[]{:S(2)}, u32[]{:S(2)}) collective-permute-start(bf16[2,48,2304]{2,1,0:T(8,128)(2,1)S(1)} %fusion.52), channel_id=1, source_target_pairs={{0,2},{1,3},{2,4},{3,5},{4,6},{5,7},{6,0},{7,1},{8,10},{9,11},{10,... | collective-permute-start | bytes 1327112 | tf_op jit(solution)/shard_map/ppermute | solution.py:282
  458.3 21.6 %collective-permute-start.34 = (bf16[2,48,2304]{2,1,0:T(8,128)(2,1)S(1)}, bf16[2,48,2304]{2,1,0:T(8,128)(2,1)S(1)}, u32[]{:S(2)}, u32[]{:S(2)}) collective-permute-start(bf16[2,48,2304]{2,1,0:T(8,128)(2,1)S(1)} %fusion.54), channel_id=1, source_target_pairs={{0,2},{1,3},{2,4},{3,5},{4,6},{5,7},{6,0},{7,1},{8,10},{9,11},{10,... | collective-permute-start | bytes 1327112 | tf_op jit(solution)/shard_map/ppermute | solution.py:282
  460.8 113.4 %collective-permute-start.83 = (bf16[4,192,768]{2,1,0:T(8,128)(2,1)S(1)}, bf16[4,192,768]{2,1,0:T(8,128)(2,1)S(1)}, u32[]{:S(2)}, u32[]{:S(2)}) collective-permute-start(bf16[4,192,768]{2,1,0:T(8,128)(2,1)S(1)} %dynamic-slice_bitcast_fusion.4), channel_id=1, source_target_pairs={{0,1},{1,0},{2,3},{3,2},{4,5},{5,4},{6,7},{7,6},{8,9},{9,8},{10,11... | collective-permute-start | bytes 3538952 | tf_op jit(solution)/shard_map/ppermute | solution.py:277
  462.1 114.0 %collective-permute-start.77 = (bf16[4,192,768]{2,1,0:T(8,128)(2,1)S(1)}, bf16[4,192,768]{2,1,0:T(8,128)(2,1)S(1)}, u32[]{:S(2)}, u32[]{:S(2)}) collective-permute-start(bf16[4,192,768]{2,1,0:T(8,128)(2,1)S(1)} %dynamic-slice_bitcast_fusion.5), channel_id=1, source_target_pairs={{0,1},{1,0},{2,3},{3,2},{4,5},{5,4},{6,7},{7,6},{8,9},{9,8},{10,11... | collective-permute-start | bytes 3538952 | tf_op jit(solution)/shard_map/ppermute | solution.py:277
  464.7 112.3 %collective-permute-start.70 = (bf16[4,48,3072]{2,1,0:T(8,128)(2,1)S(1)}, bf16[4,48,3072]{2,1,0:T(8,128)(2,1)S(1)}, u32[]{:S(2)}, u32[]{:S(2)}) collective-permute-start(bf16[4,48,3072]{2,1,0:T(8,128)(2,1)S(1)} %dynamic-slice_bitcast_fusion.6), channel_id=1, source_target_pairs={{0,1},{1,0},{2,3},{3,2},{4,5},{5,4},{6,7},{7,6},{8,9},{9,8},{10,11... | collective-permute-start | bytes 3538952 | tf_op jit(solution)/shard_map/ppermute | solution.py:277
  473.1 108.7 %collective-permute-start.64 = (bf16[4,48,3072]{2,1,0:T(8,128)(2,1)S(1)}, bf16[4,48,3072]{2,1,0:T(8,128)(2,1)S(1)}, u32[]{:S(2)}, u32[]{:S(2)}) collective-permute-start(bf16[4,48,3072]{2,1,0:T(8,128)(2,1)S(1)} %dynamic-slice_bitcast_fusion.7), channel_id=1, source_target_pairs={{0,1},{1,0},{2,3},{3,2},{4,5},{5,4},{6,7},{7,6},{8,9},{9,8},{10,11... | collective-permute-start | bytes 3538952 | tf_op jit(solution)/shard_map/ppermute | solution.py:277
  501.6 66.1 %collective-permute-start.42 = (bf16[48,2304]{1,0:T(8,128)(2,1)S(1)}, bf16[48,2304]{1,0:T(8,128)(2,1)S(1)}, u32[]{:S(2)}, u32[]{:S(2)}) collective-permute-start(bf16[48,2304]{1,0:T(8,128)(2,1)S(1)} %fusion.73), channel_id=1, source_target_pairs={{0,1},{1,0},{2,3},{3,2},{4,5},{5,4},{6,7},{7,6},{8,9},{9,8},{10,11... | collective-permute-start | bytes 663560 | tf_op jit(solution)/shard_map/ppermute | solution.py:277
  577.1 17.1 %collective-permute-start.78 = (bf16[192,768]{1,0:T(8,128)(2,1)S(1)}, bf16[192,768]{1,0:T(8,128)(2,1)S(1)}, u32[]{:S(2)}, u32[]{:S(2)}) collective-permute-start(bf16[192,768]{1,0:T(8,128)(2,1)S(1)} %dynamic-slice_bitcast_fusion.13), channel_id=1, source_target_pairs={{0,2},{1,3},{2,4},{3,5},{4,6},{5,7},{6,0},{7,1},{8,10},{9,11},{10,... | collective-permute-start | bytes 884744 | tf_op jit(solution)/shard_map/ppermute | solution.py:282
  581.8 18.7 %collective-permute-start.71 = (bf16[48,3072]{1,0:T(8,128)(2,1)S(1)}, bf16[48,3072]{1,0:T(8,128)(2,1)S(1)}, u32[]{:S(2)}, u32[]{:S(2)}) collective-permute-start(bf16[48,3072]{1,0:T(8,128)(2,1)S(1)} %dynamic-slice_bitcast_fusion.14), channel_id=1, source_target_pairs={{0,2},{1,3},{2,4},{3,5},{4,6},{5,7},{6,0},{7,1},{8,10},{9,11},{10,... | collective-permute-start | bytes 884744 | tf_op jit(solution)/shard_map/ppermute | solution.py:282
  582.4 24.5 %collective-permute-start.65 = (bf16[48,3072]{1,0:T(8,128)(2,1)S(1)}, bf16[48,3072]{1,0:T(8,128)(2,1)S(1)}, u32[]{:S(2)}, u32[]{:S(2)}) collective-permute-start(bf16[48,3072]{1,0:T(8,128)(2,1)S(1)} %dynamic-slice_bitcast_fusion.15), channel_id=1, source_target_pairs={{0,2},{1,3},{2,4},{3,5},{4,6},{5,7},{6,0},{7,1},{8,10},{9,11},{10,... | collective-permute-start | bytes 884744 | tf_op jit(solution)/shard_map/ppermute | solution.py:282
  582.7 24.8 %collective-permute-start.44 = (f32[48,2304]{1,0:T(8,128)S(1)}, f32[48,2304]{1,0:T(8,128)S(1)}, u32[]{:S(2)}, u32[]{:S(2)}) collective-permute-start(f32[48,2304]{1,0:T(8,128)S(1)} %fusion.71), channel_id=1, source_target_pairs={{0,8},{8,0},{1,9},{9,1},{2,10},{10,2},{3,11},{11,3},{4,12},{12,4},... | collective-permute-start | bytes 1327112 | tf_op jit(solution)/shard_map/ppermute | solution.py:277
  588.0 25.2 %collective-permute-start.85 = (bf16[192,768]{1,0:T(8,128)(2,1)S(1)}, bf16[192,768]{1,0:T(8,128)(2,1)S(1)}, u32[]{:S(2)}, u32[]{:S(2)}) collective-permute-start(bf16[192,768]{1,0:T(8,128)(2,1)S(1)} %fusion.56), channel_id=1, source_target_pairs={{0,2},{1,3},{2,4},{3,5},{4,6},{5,7},{6,0},{7,1},{8,10},{9,11},{10,... | collective-permute-start | bytes 884744 | tf_op jit(solution)/shard_map/ppermute | solution.py:282
  594.3 25.2 %collective-permute-start.79 = (bf16[192,768]{1,0:T(8,128)(2,1)S(1)}, bf16[192,768]{1,0:T(8,128)(2,1)S(1)}, u32[]{:S(2)}, u32[]{:S(2)}) collective-permute-start(bf16[192,768]{1,0:T(8,128)(2,1)S(1)} %fusion.58), channel_id=1, source_target_pairs={{0,2},{1,3},{2,4},{3,5},{4,6},{5,7},{6,0},{7,1},{8,10},{9,11},{10,... | collective-permute-start | bytes 884744 | tf_op jit(solution)/shard_map/ppermute | solution.py:282
  600.6 25.2 %collective-permute-start.72 = (bf16[48,3072]{1,0:T(8,128)(2,1)S(1)}, bf16[48,3072]{1,0:T(8,128)(2,1)S(1)}, u32[]{:S(2)}, u32[]{:S(2)}) collective-permute-start(bf16[48,3072]{1,0:T(8,128)(2,1)S(1)} %fusion.60), channel_id=1, source_target_pairs={{0,2},{1,3},{2,4},{3,5},{4,6},{5,7},{6,0},{7,1},{8,10},{9,11},{10,... | collective-permute-start | bytes 884744 | tf_op jit(solution)/shard_map/ppermute | solution.py:282
  606.9 25.2 %collective-permute-start.66 = (bf16[48,3072]{1,0:T(8,128)(2,1)S(1)}, bf16[48,3072]{1,0:T(8,128)(2,1)S(1)}, u32[]{:S(2)}, u32[]{:S(2)}) collective-permute-start(bf16[48,3072]{1,0:T(8,128)(2,1)S(1)} %fusion.62), channel_id=1, source_target_pairs={{0,2},{1,3},{2,4},{3,5},{4,6},{5,7},{6,0},{7,1},{8,10},{9,11},{10,... | collective-permute-start | bytes 884744 | tf_op jit(solution)/shard_map/ppermute | solution.py:282
  613.3 25.2 %collective-permute-start.86 = (bf16[192,768]{1,0:T(8,128)(2,1)S(1)}, bf16[192,768]{1,0:T(8,128)(2,1)S(1)}, u32[]{:S(2)}, u32[]{:S(2)}) collective-permute-start(bf16[192,768]{1,0:T(8,128)(2,1)S(1)} %fusion.55), channel_id=1, source_target_pairs={{0,2},{1,3},{2,4},{3,5},{4,6},{5,7},{6,0},{7,1},{8,10},{9,11},{10,... | collective-permute-start | bytes 884744 | tf_op jit(solution)/shard_map/ppermute | solution.py:282
  619.6 25.2 %collective-permute-start.80 = (bf16[192,768]{1,0:T(8,128)(2,1)S(1)}, bf16[192,768]{1,0:T(8,128)(2,1)S(1)}, u32[]{:S(2)}, u32[]{:S(2)}) collective-permute-start(bf16[192,768]{1,0:T(8,128)(2,1)S(1)} %fusion.57), channel_id=1, source_target_pairs={{0,2},{1,3},{2,4},{3,5},{4,6},{5,7},{6,0},{7,1},{8,10},{9,11},{10,... | collective-permute-start | bytes 884744 | tf_op jit(solution)/shard_map/ppermute | solution.py:282
  625.9 23.1 %collective-permute-start.73 = (bf16[48,3072]{1,0:T(8,128)(2,1)S(1)}, bf16[48,3072]{1,0:T(8,128)(2,1)S(1)}, u32[]{:S(2)}, u32[]{:S(2)}) collective-permute-start(bf16[48,3072]{1,0:T(8,128)(2,1)S(1)} %fusion.59), channel_id=1, source_target_pairs={{0,2},{1,3},{2,4},{3,5},{4,6},{5,7},{6,0},{7,1},{8,10},{9,11},{10,... | collective-permute-start | bytes 884744 | tf_op jit(solution)/shard_map/ppermute | solution.py:282
  632.2 19.9 %collective-permute-start.67 = (bf16[48,3072]{1,0:T(8,128)(2,1)S(1)}, bf16[48,3072]{1,0:T(8,128)(2,1)S(1)}, u32[]{:S(2)}, u32[]{:S(2)}) collective-permute-start(bf16[48,3072]{1,0:T(8,128)(2,1)S(1)} %fusion.61), channel_id=1, source_target_pairs={{0,2},{1,3},{2,4},{3,5},{4,6},{5,7},{6,0},{7,1},{8,10},{9,11},{10,... | collective-permute-start | bytes 884744 | tf_op jit(solution)/shard_map/ppermute | solution.py:282
  638.6 15.2 %collective-permute-start.87 = (bf16[192,768]{1,0:T(8,128)(2,1)S(1)}, bf16[192,768]{1,0:T(8,128)(2,1)S(1)}, u32[]{:S(2)}, u32[]{:S(2)}) collective-permute-start(bf16[192,768]{1,0:T(8,128)(2,1)S(1)} %fusion.68), channel_id=1, source_target_pairs={{0,16},{16,0},{1,17},{17,1},{2,18},{18,2},{3,19},{19,3},{4,20},{20... | collective-permute-start | bytes 884744 | tf_op jit(solution)/shard_map/ppermute | solution.py:347
  (90 other events, 834.9 us)

commit v2 on v1

--- a/solution.py
+++ b/solution.py
@@ -213,7 +213,7 @@
     return (output, stored)
 
 
-def layer_backward(gradient, stored, seq_lengths, matrices, vectors):
+def layer_backward(gradient, stored, seq_lengths, matrices, vectors, sums, layer):
     (
         inputs,
         projected,
@@ -234,28 +234,33 @@
     second_gain_term = jnp.sum(gradient * normed_second, axis=0)
     second_shift_term = jnp.sum(gradient, axis=0)
     grad_branch_two = grad_second.astype(LOWER)
+
+    def begin(index, left, right, pauses):
+        product = over_contract(left, right, 0, 0).astype(LOWER)
+        sums.start((layer, index), sum_rows(product, index == 0, pauses))
+
+    begin(3, activation, grad_branch_two, (0, 1))
+    grad_second, grad_branch_two = sums.boundary(grad_second, grad_branch_two)
     reduce_bias_term = jnp.sum(grad_branch_two.astype(WIDE), axis=0)
     grad_preact = (times_transposed(grad_branch_two, reduce_matrix) * slope).astype(LOWER)
+    begin(2, normal_low, grad_preact, (1, 1))
+    grad_second, grad_preact = sums.boundary(grad_second, grad_preact)
     expand_bias_term = jnp.sum(grad_preact.astype(WIDE), axis=0)
     grad_normal = grad_second + times_transposed(grad_preact, expand_matrix)
     grad_first = norm_backward(grad_normal, normed_first, inverse_first, first_gain)
     first_gain_term = jnp.sum(grad_normal * normed_first, axis=0)
     first_shift_term = jnp.sum(grad_normal, axis=0)
     grad_branch_one = grad_first.astype(LOWER)
+    begin(1, attended, grad_branch_one, (1, 0))
+    grad_first, grad_branch_one = sums.boundary(grad_first, grad_branch_one)
     output_bias_term = jnp.sum(grad_branch_one.astype(WIDE), axis=0)
     grad_attended = times_transposed(grad_branch_one, output_matrix).astype(LOWER)
     grad_projected = attention_backward(projected, grad_attended, seq_lengths)
+    begin(0, inputs, grad_projected, (0, 0))
+    grad_first, grad_projected = sums.boundary(grad_first, grad_projected)
     column_sums = jnp.sum(grad_projected.astype(WIDE), axis=0)
     grad_inputs = grad_first + times_transposed(grad_projected, joint_matrix)
-    products = tuple(
-        over_contract(left, right, 0, 0).astype(LOWER)
-        for left, right in (
-            (inputs, grad_projected),
-            (attended, grad_branch_one),
-            (normal_low, grad_preact),
-            (activation, grad_branch_two),
-        )
-    )
+    (grad_inputs,) = sums.boundary(grad_inputs)
     vector_terms = jnp.concatenate(
         [
             column_sums[:model_width],
@@ -269,7 +274,7 @@
             expand_bias_term,
         ]
     )
-    return (grad_inputs, products, vector_terms)
+    return (grad_inputs, vector_terms)
 
 
 def swap(array, axis, distance=1):
@@ -292,13 +297,17 @@
     return lax.dynamic_index_in_dim(array, place, axis, keepdims=False)
 
 
-def gather_rows(rows, pair_first):
+def after(value, *others):
+    return lax.optimization_barrier((value,) + others)[0]
+
+
+def gather_rows(rows, pair_first, *others):
     size = lax.axis_size("grid")
     steps = size // 2
     here = lax.axis_index("grid")
     column, side = here // 2, here % 2
     buffer = jnp.zeros((steps, 2) + rows.shape, rows.dtype)
-    moving = rows
+    moving = after(rows, *others) if others else rows
     if pair_first:
         pair = jnp.zeros((2,) + rows.shape, rows.dtype)
         moving = put(put(pair, rows, side), swap(rows, "grid"), 1 - side)
@@ -310,12 +319,14 @@
             buffer = put(buffer, moving, place, side)
             buffer = put(buffer, swap(moving, "grid"), place, 1 - side)
         if step < steps - 1:
+            last_sent = moving
             moving = onward(moving)
-    return buffer.reshape(size * rows.shape[0], rows.shape[1])
+    return buffer.reshape(size * rows.shape[0], rows.shape[1]), last_sent
 
 
 def pair_sum(array, side, axis):
-    received = swap(pick(array, 1 - side, axis).astype(LOWER), "grid")
+    sent = yield pick(array, 1 - side, axis).astype(LOWER)
+    received = swap(sent, "grid")
     return pick(array, side, axis).astype(WIDE) + received.astype(WIDE)
 
 
@@ -323,30 +334,76 @@
     steps = array.shape[0]
     moving = pick(array, (column - 1) % steps).astype(WIDE)
     for step in range(steps - 1):
-        received = onward(moving.astype(LOWER))
+        sent = yield moving.astype(LOWER)
+        received = onward(sent)
         moving = received.astype(WIDE) + pick(array, (column - 2 - step) % steps).astype(WIDE)
     return moving
 
 
-def sum_rows(product, pair_last):
+def pause(count):
+    for _ in range(count):
+        yield None
+
+
+def sum_rows(product, pair_last, pauses):
     size = lax.axis_size("grid")
     core = lax.axis_index("section")
     here = lax.axis_index("grid")
     column, side = here // 2, here % 2
     rows, width = product.shape
     halves = product.reshape(size // 2, 2, 2, rows // size // 2, width)
-    received = swap(pick(halves, 1 - core, 2), "section")
+    sent = yield pick(halves, 1 - core, 2)
+    received = swap(sent, "section")
+    yield from pause(pauses[0])
     both = (pick(halves, core, 2).astype(WIDE) + received.astype(WIDE)).astype(LOWER)
     if pair_last:
-        total = pair_sum(ring_sum(both, column), side, 0)
+        ring = yield from ring_sum(both, column)
+        yield from pause(pauses[1])
+        total = yield from pair_sum(ring, side, 0)
     else:
-        total = ring_sum(pair_sum(both, side, 1).astype(LOWER), column)
+        pair = yield from pair_sum(both, side, 1)
+        yield from pause(pauses[1])
+        total = yield from ring_sum(pair.astype(LOWER), column)
     groups = lax.axis_size("dp")
-    sent = total.astype(LOWER)
+    sent = yield total.astype(LOWER)
     for step in range(1, groups):
         received = lax.ppermute(sent, "dp", [(i, (i + step) % groups) for i in range(groups)])
         total = total + received.astype(WIDE)
     return total
+
+
+class Sums:
+    def __init__(self):
+        self.running = {}
+        self.pending = {}
+        self.results = {}
+
+    def resume(self, name, value):
+        try:
+            self.pending[name] = self.running[name].send(value)
+        except StopIteration as stop:
+            self.results[name] = stop.value
+            del self.running[name]
+            self.pending.pop(name, None)
+
+    def start(self, name, generator):
+        self.running[name] = generator
+        self.resume(name, None)
+
+    def boundary(self, *values):
+        names = list(self.running)
+        given = [self.pending[name] for name in names]
+        held = [value for value in given if value is not None]
+        tied = lax.optimization_barrier(tuple(values) + tuple(held))
+        passed = list(tied[len(values) :])
+        for name, value in zip(names, given):
+            self.resume(name, None if value is None else passed.pop(0))
+        return tied[: len(values)]
+
+    def finish(self):
+        while self.running:
+            for name in list(self.running):
+                self.resume(name, self.pending[name])
 
 
 def on_device(
@@ -400,12 +457,16 @@
         jnp.split(layer, cuts[:-1])
         for layer in both_layers(jnp.concatenate([v[0] for v in vector_list]))
     ]
+    joint_rows, joint_sent = gather_rows(joint_weight[0], True)
+    output_rows, output_sent = gather_rows(output_weight[0], False)
+    expand_rows, expand_sent = gather_rows(expand_weight[0], False, joint_sent, output_sent)
+    reduce_rows, _ = gather_rows(reduce_weight[0], False, expand_sent)
     matrix_layers = list(
         zip(
-            both_layers(gather_rows(joint_weight[0], True)),
-            both_layers(gather_rows(output_weight[0], False)),
-            both_layers(gather_rows(expand_weight[0], False)),
-            both_layers(gather_rows(reduce_weight[0], False)),
+            both_layers(joint_rows),
+            both_layers(output_rows),
+            both_layers(expand_rows),
+            both_layers(reduce_rows),
         )
     )
     stored_list = []
@@ -416,19 +477,21 @@
         stored_list.append(stored)
         hidden = output.astype(LOWER)
     gradient = cotangent.astype(WIDE)
-    sums = [None, None]
+    sums = Sums()
     vector_terms = [None, None]
     for layer in (1, 0):
-        gradient, products, vector_terms[layer] = layer_backward(
+        gradient, vector_terms[layer] = layer_backward(
             gradient,
             stored_list[layer],
             seq_lengths,
             matrix_layers[layer],
             vector_layers[layer],
+            sums,
+            layer,
         )
-        sums[layer] = [sum_rows(products[i], i == 0) for i in range(4)]
         if layer == 1:
             gradient = gradient.astype(LOWER).astype(WIDE)
+    sums.finish()
     own_rows = jnp.where(first_core, gradient, output)
     other_rows = swap(jnp.where(first_core, output, gradient), "section")
     boundary = put(put(jnp.zeros((2,) + own_rows.shape, WIDE), own_rows, core), other_rows, 1 - core)
@@ -437,7 +500,7 @@
     factor = 1.0 / math.sqrt(micro_count * row_count * positions)
     matrix_grads = []
     for index in range(4):
-        first_half, second_half = sums[0][index], sums[1][index]
+        first_half, second_half = sums.results[0, index], sums.results[1, index]
         kept = jnp.where(first_core, first_half, second_half)
         received = swap(jnp.where(first_core, second_half, first_half), "section")
         whole = put(put(jnp.zeros((2,) + kept.shape, WIDE), kept, core), received, 1 - core)

time: 672 us -> 647 us (0.963)
  waiting for transfers between devices: 368 us -> 349 us
  other arithmetic: 28 us -> 43.3 us
  matrix products: 95.3 us -> 81.8 us
  local copies, waits for them, and re-layouts: 58.7 us -> 51 us
    ppermute x45, waiting for transfers between devices: 128 us -> 110 us  [swap(): return lax.ppermute(array, axis, [(i, i ^ distance) for i in range(length)])]
    dot_general x8, matrix products: 31.2 us -> 20.4 us  [over_contract(): lax.dot_general(left, right, (((left_dim,), (right_dim,)), ((), ())), pre...]
    unnamed x122 -> x128, local copies, waits for them, and re-layouts: 27.8 us -> 19.9 us
    ppermute x36, waiting for transfers between devices: 233 us -> 226 us  [onward(): lax.ppermute(array, 'grid', [(i, (i + 2) % length) for i in range(length)])]
  transfers between devices with their start and end apart: 89 -> 89, of which waited for: 49 -> 48; matrix products, arithmetic and copies ran while one was open for 11% -> 18% of each run, Pallas kernels for 2% -> 7%
where the time goes in v2:
time: 647 us; the launch traced here: 640 us
  waiting for transfers between devices  349 us (54%)
  matrix products  81.8 us (13%)
  Pallas kernels  56.3 us (9%)
  starting transfers between devices  55.8 us (9%)
  local copies, waits for them, and re-layouts  51 us (8%)
  other arithmetic  43.3 us (7%)
    ppermute x36, waiting for transfers between devices, onward(): lax.ppermute(array, 'grid', [(i, (i + 2) % length) for i in range(length)])  226 us
    ppermute x45, waiting for transfers between devices, swap(): return lax.ppermute(array, axis, [(i, i ^ distance) for i in range(length)])  110 us
    pallas_call x2, Pallas kernels, attention_backward(): pl.pallas_call(kernel, grid=(seq_count, pairs), in_specs=[pl.BlockSpec(me...  34.6 us
    dot_general x8, matrix products, times_transposed(): lax.dot_general(left_rows, right_rows, (((1,), (1,)), ((), ())), preferre...  30.2 us
    ppermute x45, starting transfers between devices, swap(): return lax.ppermute(array, axis, [(i, i ^ distance) for i in range(length)])  28.4 us
    pallas_call x2, Pallas kernels, attention(): pl.pallas_call(kernel, grid=(seq_count, pairs), in_specs=[pl.BlockSpec(me...  21.7 us
    dot_general x8, matrix products, over_contract(): lax.dot_general(left, right, (((left_dim,), (right_dim,)), ((), ())), pre...  20.4 us
    unnamed x128, local copies, waits for them, and re-layouts  19.9 us
  transfers between devices with their start and end apart: 89, of which 48 were waited for; matrix products, arithmetic and copies ran while one was open for 18% of the time, Pallas kernels for 7%

profile of v2, /device:TPU:0, one launch (start us, length us, event | category | flops | bytes accessed | tf_op | source)
XLA Modules:
  0.0 640.0 jit_solution(1487785080415134278)
XLA Ops:
  0.7 3.0 collective-permute-start.7
  32.3 16.4 %collective-permute-done.2 = bf16[2,96,2304]{2,1,0:T(8,128)(2,1)S(1)} collective-permute-done((bf16[2,96,2304]{2,1,0:T(8,128)(2,1)S(1)}, bf16[2,96,2304]{2,1,0:T(8,128)(2,1)S(1)}, u32[]{:S(2)}, u32[]{:S(2)}) %collective-permute-start.2) | collective-permute-done | bytes 884768 | tf_op jit(solution)/shard_map/ppermute | solution.py:287
  51.5 19.9 %collective-permute-done.3 = bf16[2,96,2304]{2,1,0:T(8,128)(2,1)S(1)} collective-permute-done((bf16[2,96,2304]{2,1,0:T(8,128)(2,1)S(1)}, bf16[2,96,2304]{2,1,0:T(8,128)(2,1)S(1)}, u32[]{:S(2)}, u32[]{:S(2)}) %collective-permute-start.3) | collective-permute-done | bytes 884768 | tf_op jit(solution)/shard_map/ppermute | solution.py:287
  74.0 16.9 %collective-permute-done.16 = bf16[96,3072]{1,0:T(8,128)(2,1)S(1)} collective-permute-done((bf16[96,3072]{1,0:T(8,128)(2,1)S(1)}, bf16[96,3072]{1,0:T(8,128)(2,1)S(1)}, u32[]{:S(2)}, u32[]{:S(2)}) %collective-permute-start.16) | collective-permute-done | bytes 589856 | tf_op jit(solution)/shard_map/ppermute | solution.py:287
  91.6 18.3 %collective-permute-done.4 = bf16[2,96,2304]{2,1,0:T(8,128)(2,1)S(1)} collective-permute-done((bf16[2,96,2304]{2,1,0:T(8,128)(2,1)S(1)}, bf16[2,96,2304]{2,1,0:T(8,128)(2,1)S(1)}, u32[]{:S(2)}, u32[]{:S(2)}) %collective-permute-start.4) | collective-permute-done | bytes 884768 | tf_op jit(solution)/shard_map/ppermute | solution.py:287
  110.0 9.7 %collective-permute-done.18 = bf16[96,3072]{1,0:T(8,128)(2,1)S(1)} collective-permute-done((bf16[96,3072]{1,0:T(8,128)(2,1)S(1)}, bf16[96,3072]{1,0:T(8,128)(2,1)S(1)}, u32[]{:S(2)}, u32[]{:S(2)}) %collective-permute-start.18) | collective-permute-done | bytes 589856 | tf_op jit(solution)/shard_map/ppermute | solution.py:287
  122.2 13.7 %collective-permute-done.23 = bf16[384,768]{1,0:T(8,128)(2,1)S(1)} collective-permute-done((bf16[384,768]{1,0:T(8,128)(2,1)S(1)}, bf16[384,768]{1,0:T(8,128)(2,1)S(1)}, u32[]{:S(2)}, u32[]{:S(2)}) %collective-permute-start.23) | collective-permute-done | bytes 589856 | tf_op jit(solution)/shard_map/ppermute | solution.py:282
  139.9 8.7 %collective-permute-done.19 = bf16[96,3072]{1,0:T(8,128)(2,1)S(1)} collective-permute-done((bf16[96,3072]{1,0:T(8,128)(2,1)S(1)}, bf16[96,3072]{1,0:T(8,128)(2,1)S(1)}, u32[]{:S(2)}, u32[]{:S(2)}) %collective-permute-start.19) | collective-permute-done | bytes 589856 | tf_op jit(solution)/shard_map/ppermute | solution.py:282
  150.7 9.6 %collective-permute-done.26 = bf16[384,768]{1,0:T(8,128)(2,1)S(1)} collective-permute-done((bf16[384,768]{1,0:T(8,128)(2,1)S(1)}, bf16[384,768]{1,0:T(8,128)(2,1)S(1)}, u32[]{:S(2)}, u32[]{:S(2)}) %collective-permute-start.26) | collective-permute-done | bytes 589856 | tf_op jit(solution)/shard_map/ppermute | solution.py:287
  161.0 12.9 %collective-permute-done.21 = bf16[96,3072]{1,0:T(8,128)(2,1)S(1)} collective-permute-done((bf16[96,3072]{1,0:T(8,128)(2,1)S(1)}, bf16[96,3072]{1,0:T(8,128)(2,1)S(1)}, u32[]{:S(2)}, u32[]{:S(2)}) %collective-permute-start.21) | collective-permute-done | bytes 589856 | tf_op jit(solution)/shard_map/ppermute | solution.py:282
  174.1 11.5 %collective-permute-done.28 = bf16[384,768]{1,0:T(8,128)(2,1)S(1)} collective-permute-done((bf16[384,768]{1,0:T(8,128)(2,1)S(1)}, bf16[384,768]{1,0:T(8,128)(2,1)S(1)}, u32[]{:S(2)}, u32[]{:S(2)}) %collective-permute-start.28) | collective-permute-done | bytes 589856 | tf_op jit(solution)/shard_map/ppermute | solution.py:287
  187.8 9.1 %collective-permute-done.29 = bf16[384,768]{1,0:T(8,128)(2,1)S(1)} collective-permute-done((bf16[384,768]{1,0:T(8,128)(2,1)S(1)}, bf16[384,768]{1,0:T(8,128)(2,1)S(1)}, u32[]{:S(2)}, u32[]{:S(2)}) %collective-permute-start.29) | collective-permute-done | bytes 589856 | tf_op jit(solution)/shard_map/ppermute | solution.py:282
  202.6 3.9 collective-permute-done.11
  216.6 11.1 %shard_map.254 = bf16[512,768]{1,0:T(8,128)(2,1)S(1)} custom-call(s32[1]{0:T(128)} %bitcast.2.refs_0_, bf16[512,2304]{1,0:T(8,128)(2,1)S(1)} %fusion.16.refs_1_.refs_2_.refs_3_, bf16[512,2304]{1,0:T(8,128)(2,1)S(1)} %fusion.16.refs_1_.refs_2_.refs_3_, bf16[512,2304]{1,0:T(8,128)(2,1)S(1)} %fusion.16.refs_1_.refs_2_.refs_3_), custom_call_target="tpu_custom_call" | custom-call | flops 1610612736 | bytes 3145728 | tf_op jit(solution)/shard_map/pallas_call | solution.py:118
  230.7 5.8 multiply_convert_fusion.1
  236.5 5.0 fusion.97
  244.1 10.7 %shard_map.255 = bf16[512,768]{1,0:T(8,128)(2,1)S(1)} custom-call(s32[1]{0:T(128)} %bitcast.2.refs_0_, bf16[512,2304]{1,0:T(8,128)(2,1)S(1)} %fusion.17.refs_1_.refs_2_.refs_3_, bf16[512,2304]{1,0:T(8,128)(2,1)S(1)} %fusion.17.refs_1_.refs_2_.refs_3_, bf16[512,2304]{1,0:T(8,128)(2,1)S(1)} %fusion.17.refs_1_.refs_2_.refs_3_), custom_call_target="tpu_custom_call" | custom-call | flops 1610612736 | bytes 3145728 | tf_op jit(solution)/shard_map/pallas_call | solution.py:118
  257.1 6.1 multiply_convert_fusion
  263.1 6.3 fusion.99
  275.9 8.5 %fusion.5 = bf16[512,3072]{1,0:T(8,128)(2,1)} fusion(f32[512,3072]{1,0:T(8,128)} %get-tuple-element.192, bf16[512,768]{1,0:T(8,128)(2,1)S(1)} %get-tuple-element.71, f32[3072]{0:T(1024)S(1)} %split.122, bf16[3072,768]{1,0:T(8,128)(2,1)} %collective-permute-done.30, bf16[3072,768]{1,0:T(8,128)(2,1)S(1)} %bitcast.343, pred[]{:T(512)S(6)} %eq.64), kind=kOutput, calls=%fused_computation.7 | convolution fusion | flops 2435579904 | bytes 19673088 | tf_op jit(solution)/shard_map/dot_general | solution.py:37
  284.5 5.3 convolution_convert_fusion.4
  298.3 5.2 fusion.32
  309.5 17.4 %shard_map.256 = bf16[512,2304]{1,0:T(8,128)(2,1)S(1)} custom-call(s32[1]{0:T(128)} %bitcast.2.refs_0_, bf16[512,2304]{1,0:T(8,128)(2,1)S(1)} %fusion.17.refs_1_.refs_2_.refs_3_, bf16[512,2304]{1,0:T(8,128)(2,1)S(1)} %fusion.17.refs_1_.refs_2_.refs_3_, bf16[512,2304]{1,0:T(8,128)(2,1)S(1)} %fusion.17.refs_1_.refs_2_.refs_3_, ...), custom_call_target="tpu_custom_call" | custom-call | flops 4026531840 | bytes 5505024 | tf_op jit(solution)/shard_map/pallas_call | solution.py:149
  334.3 3.4 fusion.14
  342.4 6.9 %collective-permute-done.34 = bf16[192,768]{1,0:T(8,128)(2,1)S(1)} collective-permute-done((bf16[192,768]{1,0:T(8,128)(2,1)S(1)}, bf16[192,768]{1,0:T(8,128)(2,1)S(1)}, u32[]{:S(2)}, u32[]{:S(2)}) %collective-permute-start.34) | collective-permute-done | bytes 294944 | tf_op jit(solution)/shard_map/ppermute | solution.py:287
  349.3 17.8 %collective-permute-done.38 = bf16[4,48,3072]{2,1,0:T(8,128)(2,1)S(1)} collective-permute-done((bf16[4,48,3072]{2,1,0:T(8,128)(2,1)S(1)}, bf16[4,48,3072]{2,1,0:T(8,128)(2,1)S(1)}, u32[]{:S(2)}, u32[]{:S(2)}) %collective-permute-start.38) | collective-permute-done | bytes 1179680 | tf_op jit(solution)/shard_map/ppermute | solution.py:282
  377.4 3.4 collective-permute-done.37
  380.8 7.7 %collective-permute-done.40 = bf16[2,48,2304]{2,1,0:T(8,128)(2,1)S(1)} collective-permute-done((bf16[2,48,2304]{2,1,0:T(8,128)(2,1)S(1)}, bf16[2,48,2304]{2,1,0:T(8,128)(2,1)S(1)}, u32[]{:S(2)}, u32[]{:S(2)}) %collective-permute-start.40) | collective-permute-done | bytes 442400 | tf_op jit(solution)/shard_map/ppermute | solution.py:287
  393.9 6.6 %fusion.11 = bf16[512,3072]{1,0:T(8,128)(2,1)S(1)} fusion(f32[512,3072]{1,0:T(8,128)} %get-tuple-element.186, bf16[512,768]{1,0:T(8,128)(2,1)S(1)} %get-tuple-element.90, f32[3072]{0:T(1024)S(1)} %split.113, bf16[3072,768]{1,0:T(8,128)(2,1)S(1)} %bitcast.346, bf16[3072,768]{1,0:T(8,128)(2,1)} %collective-permute-done.30, pred[]{:T(512)S(6)} %eq.64), kind=kOutput, calls=%fused_computation.13 | convolution fusion | flops 2435579904 | bytes 19673088 | tf_op jit(solution)/shard_map/dot_general | solution.py:37
  400.6 3.4 convolution_convert_fusion.1
  408.5 6.6 %collective-permute-done.44 = bf16[2,48,2304]{2,1,0:T(8,128)(2,1)S(1)} collective-permute-done((bf16[2,48,2304]{2,1,0:T(8,128)(2,1)S(1)}, bf16[2,48,2304]{2,1,0:T(8,128)(2,1)S(1)}, u32[]{:S(2)}, u32[]{:S(2)}) %collective-permute-start.44) | collective-permute-done | bytes 442400 | tf_op jit(solution)/shard_map/ppermute | solution.py:287
  428.3 8.7 %collective-permute-done.47 = bf16[48,768]{1,0:T(8,128)(2,1)S(1)} collective-permute-done((bf16[48,768]{1,0:T(8,128)(2,1)S(1)}, bf16[48,768]{1,0:T(8,128)(2,1)S(1)}, u32[]{:S(2)}, u32[]{:S(2)}) %collective-permute-start.47) | collective-permute-done | bytes 73760 | tf_op jit(solution)/shard_map/ppermute | solution.py:287
  437.9 7.4 %collective-permute-done.48 = bf16[2,48,2304]{2,1,0:T(8,128)(2,1)S(1)} collective-permute-done((bf16[2,48,2304]{2,1,0:T(8,128)(2,1)S(1)}, bf16[2,48,2304]{2,1,0:T(8,128)(2,1)S(1)}, u32[]{:S(2)}, u32[]{:S(2)}) %collective-permute-start.48) | collective-permute-done | bytes 442400 | tf_op jit(solution)/shard_map/ppermute | solution.py:287
  448.2 17.1 %shard_map.257 = bf16[512,2304]{1,0:T(8,128)(2,1)S(1)} custom-call(s32[1]{0:T(128)} %bitcast.2.refs_0_, bf16[512,2304]{1,0:T(8,128)(2,1)S(1)} %fusion.16.refs_1_.refs_2_.refs_3_, bf16[512,2304]{1,0:T(8,128)(2,1)S(1)} %fusion.16.refs_1_.refs_2_.refs_3_, bf16[512,2304]{1,0:T(8,128)(2,1)S(1)} %fusion.16.refs_1_.refs_2_.refs_3_, ...), custom_call_target="tpu_custom_call" | custom-call | flops 4026531840 | bytes 5505024 | tf_op jit(solution)/shard_map/pallas_call | solution.py:149
  469.3 3.1 collective-permute-done.50
  474.5 3.1 collective-permute-done.49
  499.8 3.3 collective-permute-done.69
  504.6 18.2 %collective-permute-done.77 = bf16[4,48,3072]{2,1,0:T(8,128)(2,1)S(1)} collective-permute-done((bf16[4,48,3072]{2,1,0:T(8,128)(2,1)S(1)}, bf16[4,48,3072]{2,1,0:T(8,128)(2,1)S(1)}, u32[]{:S(2)}, u32[]{:S(2)}) %collective-permute-start.77) | collective-permute-done | bytes 1179680 | tf_op jit(solution)/shard_map/ppermute | solution.py:282
  535.4 8.0 %collective-permute-done.79 = bf16[48,3072]{1,0:T(8,128)(2,1)S(1)} collective-permute-done((bf16[48,3072]{1,0:T(8,128)(2,1)S(1)}, bf16[48,3072]{1,0:T(8,128)(2,1)S(1)}, u32[]{:S(2)}, u32[]{:S(2)}) %collective-permute-start.79) | collective-permute-done | bytes 294944 | tf_op jit(solution)/shard_map/ppermute | solution.py:287
  544.7 10.6 %collective-permute-done.80 = bf16[48,3072]{1,0:T(8,128)(2,1)S(1)} collective-permute-done((bf16[48,3072]{1,0:T(8,128)(2,1)S(1)}, bf16[48,3072]{1,0:T(8,128)(2,1)S(1)}, u32[]{:S(2)}, u32[]{:S(2)}) %collective-permute-start.80) | collective-permute-done | bytes 294944 | tf_op jit(solution)/shard_map/ppermute | solution.py:287
  555.4 6.1 collective-permute-done.71
  561.6 10.9 %collective-permute-done.72 = bf16[48,768]{1,0:T(8,128)(2,1)S(1)} collective-permute-done((bf16[48,768]{1,0:T(8,128)(2,1)S(1)}, bf16[48,768]{1,0:T(8,128)(2,1)S(1)}, u32[]{:S(2)}, u32[]{:S(2)}) %collective-permute-start.72) | collective-permute-done | bytes 73760 | tf_op jit(solution)/shard_map/ppermute | solution.py:287
  575.3 6.0 collective-permute-done.73
  582.1 10.5 %collective-permute-done.85 = bf16[192,768]{1,0:T(8,128)(2,1)S(1)} collective-permute-done((bf16[192,768]{1,0:T(8,128)(2,1)S(1)}, bf16[192,768]{1,0:T(8,128)(2,1)S(1)}, u32[]{:S(2)}, u32[]{:S(2)}) %collective-permute-start.85) | collective-permute-done | bytes 294944 | tf_op jit(solution)/shard_map/ppermute | solution.py:287
  601.3 6.6 %collective-permute-done.86 = bf16[192,768]{1,0:T(8,128)(2,1)S(1)} collective-permute-done((bf16[192,768]{1,0:T(8,128)(2,1)S(1)}, bf16[192,768]{1,0:T(8,128)(2,1)S(1)}, u32[]{:S(2)}, u32[]{:S(2)}) %collective-permute-start.86) | collective-permute-done | bytes 294944 | tf_op jit(solution)/shard_map/ppermute | solution.py:370
  609.8 13.2 %collective-permute-done.60 = bf16[2,48,2304]{2,1,0:T(8,128)(2,1)S(1)} collective-permute-done((bf16[2,48,2304]{2,1,0:T(8,128)(2,1)S(1)}, bf16[2,48,2304]{2,1,0:T(8,128)(2,1)S(1)}, u32[]{:S(2)}, u32[]{:S(2)}) %collective-permute-start.60) | collective-permute-done | bytes 442400 | tf_op jit(solution)/shard_map/ppermute | solution.py:287
  624.8 5.5 collective-permute-done.61
  632.2 4.3 collective-permute-done.62
  (491 shorter events, 203.7 us)
Async XLA Ops:
  0.7 196.4 %collective-permute-start.7 = (bf16[96,768]{1,0:T(8,128)(2,1)}, bf16[96,768]{1,0:T(8,128)(2,1)}, u32[]{:S(2)}, u32[]{:S(2)}) collective-permute-start(bf16[96,768]{1,0:T(8,128)(2,1)} %bitcast.380), channel_id=1, source_target_pairs={{0,1},{1,0},{2,3},{3,2},{4,5},{5,4},{6,7},{7,6},{8,9},{9,8},{10,11... | collective-permute-start | bytes 442376 | tf_op jit(solution)/shard_map/ppermute | solution.py:282
  3.7 27.0 %collective-permute-start.8 = (bf16[96,768]{1,0:T(8,128)(2,1)}, bf16[96,768]{1,0:T(8,128)(2,1)}, u32[]{:S(2)}, u32[]{:S(2)}) collective-permute-start(bf16[96,768]{1,0:T(8,128)(2,1)} %bitcast.381), channel_id=1, source_target_pairs={{0,2},{1,3},{2,4},{3,5},{4,6},{5,7},{6,0},{7,1},{8,10},{9,11},{10,... | collective-permute-start | bytes 442376 | tf_op jit(solution)/shard_map/ppermute | solution.py:287
  5.3 19.1 %collective-permute-start.1 = (bf16[96,2304]{1,0:T(8,128)(2,1)}, bf16[96,2304]{1,0:T(8,128)(2,1)S(1)}, u32[]{:S(2)}, u32[]{:S(2)}) collective-permute-start(bf16[96,2304]{1,0:T(8,128)(2,1)} %bitcast.378), channel_id=1, source_target_pairs={{0,1},{1,0},{2,3},{3,2},{4,5},{5,4},{6,7},{7,6},{8,9},{9,8},{10,11... | collective-permute-start | bytes 1327112 | tf_op jit(solution)/shard_map/ppermute | solution.py:282
  24.4 24.3 %collective-permute-start.2 = (bf16[2,96,2304]{2,1,0:T(8,128)(2,1)S(1)}, bf16[2,96,2304]{2,1,0:T(8,128)(2,1)S(1)}, u32[]{:S(2)}, u32[]{:S(2)}) collective-permute-start(bf16[2,96,2304]{2,1,0:T(8,128)(2,1)S(1)} %bitcast_dynamic-update-slice_fusion.28), channel_id=1, source_target_pairs={{0,2},{1,3},{2,4},{3,5},{4,6},{5,7},{6,0},{7,1},{8,10},{9,11},{10,... | collective-permute-start | bytes 2654216 | tf_op jit(solution)/shard_map/ppermute | solution.py:287
  30.7 20.8 %collective-permute-start.10 = (bf16[96,768]{1,0:T(8,128)(2,1)}, bf16[96,768]{1,0:T(8,128)(2,1)S(1)}, u32[]{:S(2)}, u32[]{:S(2)}) collective-permute-start(bf16[96,768]{1,0:T(8,128)(2,1)} %collective-permute-done.8), channel_id=1, source_target_pairs={{0,2},{1,3},{2,4},{3,5},{4,6},{5,7},{6,0},{7,1},{8,10},{9,11},{10,... | collective-permute-start | bytes 442376 | tf_op jit(solution)/shard_map/ppermute | solution.py:287
  48.7 22.7 %collective-permute-start.3 = (bf16[2,96,2304]{2,1,0:T(8,128)(2,1)S(1)}, bf16[2,96,2304]{2,1,0:T(8,128)(2,1)S(1)}, u32[]{:S(2)}, u32[]{:S(2)}) collective-permute-start(bf16[2,96,2304]{2,1,0:T(8,128)(2,1)S(1)} %collective-permute-done.2), channel_id=1, source_target_pairs={{0,2},{1,3},{2,4},{3,5},{4,6},{5,7},{6,0},{7,1},{8,10},{9,11},{10,... | collective-permute-start | bytes 2654216 | tf_op jit(solution)/shard_map/ppermute | solution.py:287
  71.4 20.1 %collective-permute-start.15 = (bf16[96,3072]{1,0:T(8,128)(2,1)S(1)}, bf16[96,3072]{1,0:T(8,128)(2,1)S(1)}, u32[]{:S(2)}, u32[]{:S(2)}) collective-permute-start(bf16[96,3072]{1,0:T(8,128)(2,1)S(1)} %bitcast.372), channel_id=1, source_target_pairs={{0,1},{1,0},{2,3},{3,2},{4,5},{5,4},{6,7},{7,6},{8,9},{9,8},{10,11... | collective-permute-start | bytes 1769480 | tf_op jit(solution)/shard_map/ppermute | solution.py:282
  72.9 18.1 %collective-permute-start.16 = (bf16[96,3072]{1,0:T(8,128)(2,1)S(1)}, bf16[96,3072]{1,0:T(8,128)(2,1)S(1)}, u32[]{:S(2)}, u32[]{:S(2)}) collective-permute-start(bf16[96,3072]{1,0:T(8,128)(2,1)S(1)} %bitcast.373), channel_id=1, source_target_pairs={{0,2},{1,3},{2,4},{3,5},{4,6},{5,7},{6,0},{7,1},{8,10},{9,11},{10,... | collective-permute-start | bytes 1769480 | tf_op jit(solution)/shard_map/ppermute | solution.py:287
  72.9 37.0 %collective-permute-start.4 = (bf16[2,96,2304]{2,1,0:T(8,128)(2,1)S(1)}, bf16[2,96,2304]{2,1,0:T(8,128)(2,1)S(1)}, u32[]{:S(2)}, u32[]{:S(2)}) collective-permute-start(bf16[2,96,2304]{2,1,0:T(8,128)(2,1)S(1)} %collective-permute-done.3), channel_id=1, source_target_pairs={{0,2},{1,3},{2,4},{3,5},{4,6},{5,7},{6,0},{7,1},{8,10},{9,11},{10,... | collective-permute-start | bytes 2654216 | tf_op jit(solution)/shard_map/ppermute | solution.py:287
  91.0 30.7 %collective-permute-start.17 = (bf16[96,3072]{1,0:T(8,128)(2,1)S(1)}, bf16[96,3072]{1,0:T(8,128)(2,1)S(1)}, u32[]{:S(2)}, u32[]{:S(2)}) collective-permute-start(bf16[96,3072]{1,0:T(8,128)(2,1)S(1)} %collective-permute-done.16), channel_id=1, source_target_pairs={{0,1},{1,0},{2,3},{3,2},{4,5},{5,4},{6,7},{7,6},{8,9},{9,8},{10,11... | collective-permute-start | bytes 1769480 | tf_op jit(solution)/shard_map/ppermute | solution.py:282
  91.5 28.2 %collective-permute-start.18 = (bf16[96,3072]{1,0:T(8,128)(2,1)S(1)}, bf16[96,3072]{1,0:T(8,128)(2,1)S(1)}, u32[]{:S(2)}, u32[]{:S(2)}) collective-permute-start(bf16[96,3072]{1,0:T(8,128)(2,1)S(1)} %collective-permute-done.16), channel_id=1, source_target_pairs={{0,2},{1,3},{2,4},{3,5},{4,6},{5,7},{6,0},{7,1},{8,10},{9,11},{10,... | collective-permute-start | bytes 1769480 | tf_op jit(solution)/shard_map/ppermute | solution.py:287
  119.7 16.3 %collective-permute-start.23 = (bf16[384,768]{1,0:T(8,128)(2,1)S(1)}, bf16[384,768]{1,0:T(8,128)(2,1)S(1)}, u32[]{:S(2)}, u32[]{:S(2)}) collective-permute-start(bf16[384,768]{1,0:T(8,128)(2,1)S(1)} %bitcast.375), channel_id=1, source_target_pairs={{0,1},{1,0},{2,3},{3,2},{4,5},{5,4},{6,7},{7,6},{8,9},{9,8},{10,11... | collective-permute-start | bytes 1769480 | tf_op jit(solution)/shard_map/ppermute | solution.py:282
  120.2 18.1 %collective-permute-start.24 = (bf16[384,768]{1,0:T(8,128)(2,1)S(1)}, bf16[384,768]{1,0:T(8,128)(2,1)S(1)}, u32[]{:S(2)}, u32[]{:S(2)}) collective-permute-start(bf16[384,768]{1,0:T(8,128)(2,1)S(1)} %bitcast.376), channel_id=1, source_target_pairs={{0,2},{1,3},{2,4},{3,5},{4,6},{5,7},{6,0},{7,1},{8,10},{9,11},{10,... | collective-permute-start | bytes 1769480 | tf_op jit(solution)/shard_map/ppermute | solution.py:287
  120.2 28.4 %collective-permute-start.19 = (bf16[96,3072]{1,0:T(8,128)(2,1)S(1)}, bf16[96,3072]{1,0:T(8,128)(2,1)S(1)}, u32[]{:S(2)}, u32[]{:S(2)}) collective-permute-start(bf16[96,3072]{1,0:T(8,128)(2,1)S(1)} %collective-permute-done.18), channel_id=1, source_target_pairs={{0,1},{1,0},{2,3},{3,2},{4,5},{5,4},{6,7},{7,6},{8,9},{9,8},{10,11... | collective-permute-start | bytes 1769480 | tf_op jit(solution)/shard_map/ppermute | solution.py:282
  121.7 26.9 %collective-permute-start.20 = (bf16[96,3072]{1,0:T(8,128)(2,1)S(1)}, bf16[96,3072]{1,0:T(8,128)(2,1)S(1)}, u32[]{:S(2)}, u32[]{:S(2)}) collective-permute-start(bf16[96,3072]{1,0:T(8,128)(2,1)S(1)} %collective-permute-done.18), channel_id=1, source_target_pairs={{0,2},{1,3},{2,4},{3,5},{4,6},{5,7},{6,0},{7,1},{8,10},{9,11},{10,... | collective-permute-start | bytes 1769480 | tf_op jit(solution)/shard_map/ppermute | solution.py:287
  136.0 78.5 %collective-permute-start.5 = (bf16[768,2304]{1,0:T(8,128)(2,1)S(1)}, bf16[768,2304]{1,0:T(8,128)(2,1)S(1)}, u32[]{:S(2)}, u32[]{:S(2)}) collective-permute-start(bf16[768,2304]{1,0:T(8,128)(2,1)S(1)} %bitcast.360), channel_id=1, source_target_pairs={{0,8},{8,0},{1,9},{9,1},{2,10},{10,2},{3,11},{11,3},{4,12},{12,4},... | collective-permute-start | bytes 10616840 | tf_op jit(solution)/shard_map/ppermute | solution.py:282
  138.3 35.7 %collective-permute-start.25 = (bf16[384,768]{1,0:T(8,128)(2,1)S(1)}, bf16[384,768]{1,0:T(8,128)(2,1)S(1)}, u32[]{:S(2)}, u32[]{:S(2)}) collective-permute-start(bf16[384,768]{1,0:T(8,128)(2,1)S(1)} %collective-permute-done.24), channel_id=1, source_target_pairs={{0,1},{1,0},{2,3},{3,2},{4,5},{5,4},{6,7},{7,6},{8,9},{9,8},{10,11... | collective-permute-start | bytes 1769480 | tf_op jit(solution)/shard_map/ppermute | solution.py:282
  148.6 25.3 %collective-permute-start.21 = (bf16[96,3072]{1,0:T(8,128)(2,1)S(1)}, bf16[96,3072]{1,0:T(8,128)(2,1)S(1)}, u32[]{:S(2)}, u32[]{:S(2)}) collective-permute-start(bf16[96,3072]{1,0:T(8,128)(2,1)S(1)} %collective-permute-done.20), channel_id=1, source_target_pairs={{0,1},{1,0},{2,3},{3,2},{4,5},{5,4},{6,7},{7,6},{8,9},{9,8},{10,11... | collective-permute-start | bytes 1769480 | tf_op jit(solution)/shard_map/ppermute | solution.py:282
  160.3 25.8 %collective-permute-start.27 = (bf16[384,768]{1,0:T(8,128)(2,1)S(1)}, bf16[384,768]{1,0:T(8,128)(2,1)S(1)}, u32[]{:S(2)}, u32[]{:S(2)}) collective-permute-start(bf16[384,768]{1,0:T(8,128)(2,1)S(1)} %collective-permute-done.26), channel_id=1, source_target_pairs={{0,1},{1,0},{2,3},{3,2},{4,5},{5,4},{6,7},{7,6},{8,9},{9,8},{10,11... | collective-permute-start | bytes 1769480 | tf_op jit(solution)/shard_map/ppermute | solution.py:282
  174.0 56.7 %collective-permute-start.22 = (bf16[768,3072]{1,0:T(8,128)(2,1)S(1)}, bf16[768,3072]{1,0:T(8,128)(2,1)S(1)}, u32[]{:S(2)}, u32[]{:S(2)}) collective-permute-start(bf16[768,3072]{1,0:T(8,128)(2,1)S(1)} %bitcast.347), channel_id=1, source_target_pairs={{0,8},{8,0},{1,9},{9,1},{2,10},{10,2},{3,11},{11,3},{4,12},{12,4},... | collective-permute-start | bytes 14155784 | tf_op jit(solution)/shard_map/ppermute | solution.py:282
  186.1 15.2 %collective-permute-start.9 = (bf16[96,768]{1,0:T(8,128)(2,1)}, bf16[96,768]{1,0:T(8,128)(2,1)S(1)}, u32[]{:S(2)}, u32[]{:S(2)}) collective-permute-start(bf16[96,768]{1,0:T(8,128)(2,1)} %collective-permute-done.8), channel_id=1, source_target_pairs={{0,1},{1,0},{2,3},{3,2},{4,5},{5,4},{6,7},{7,6},{8,9},{9,8},{10,11... | collective-permute-start | bytes 442376 | tf_op jit(solution)/shard_map/ppermute | solution.py:282
  197.0 39.5 %collective-permute-start.30 = (bf16[3072,768]{1,0:T(8,128)(2,1)S(1)}, bf16[3072,768]{1,0:T(8,128)(2,1)}, u32[]{:S(2)}, u32[]{:S(2)}) collective-permute-start(bf16[3072,768]{1,0:T(8,128)(2,1)S(1)} %bitcast.340), channel_id=1, source_target_pairs={{0,8},{8,0},{1,9},{9,1},{2,10},{10,2},{3,11},{11,3},{4,12},{12,4},... | collective-permute-start | bytes 14155784 | tf_op jit(solution)/shard_map/ppermute | solution.py:282
  275.7 17.6 %collective-permute-start.31 = (bf16[4,2,192,768]{3,2,1,0:T(8,128)(2,1)S(1)}, bf16[4,2,192,768]{3,2,1,0:T(8,128)(2,1)}, u32[]{:S(2)}, u32[]{:S(2)}) collective-permute-start(bf16[4,2,192,768]{3,2,1,0:T(8,128)(2,1)S(1)} %dynamic-slice_bitcast_fusion.1), channel_id=1, source_target_pairs={{0,8},{8,0},{1,9},{9,1},{2,10},{10,2},{3,11},{11,3},{4,12},{12,4},... | collective-permute-start | bytes 7077896 | tf_op jit(solution)/shard_map/ppermute | solution.py:282
  306.6 26.0 %collective-permute-start.32 = (bf16[4,192,768]{2,1,0:T(8,128)(2,1)}, bf16[4,192,768]{2,1,0:T(8,128)(2,1)}, u32[]{:S(2)}, u32[]{:S(2)}) collective-permute-start(bf16[4,192,768]{2,1,0:T(8,128)(2,1)} %dynamic-slice_bitcast_fusion.7), channel_id=1, source_target_pairs={{0,1},{1,0},{2,3},{3,2},{4,5},{5,4},{6,7},{7,6},{8,9},{9,8},{10,11... | collective-permute-start | bytes 3538952 | tf_op jit(solution)/shard_map/ppermute | solution.py:282
  308.1 26.1 %collective-permute-start.33 = (bf16[4,2,48,3072]{3,2,1,0:T(8,128)(2,1)}, bf16[4,2,48,3072]{3,2,1,0:T(8,128)(2,1)}, u32[]{:S(2)}, u32[]{:S(2)}) collective-permute-start(bf16[4,2,48,3072]{3,2,1,0:T(8,128)(2,1)} %dynamic-slice_bitcast_fusion), channel_id=1, source_target_pairs={{0,8},{8,0},{1,9},{9,1},{2,10},{10,2},{3,11},{11,3},{4,12},{12,4},... | collective-permute-start | bytes 7077896 | tf_op jit(solution)/shard_map/ppermute | solution.py:282
  308.1 22.1 %collective-permute-start.35 = (bf16[4,2,48,768]{3,2,1,0:T(8,128)(2,1)}, bf16[4,2,48,768]{3,2,1,0:T(8,128)(2,1)}, u32[]{:S(2)}, u32[]{:S(2)}) collective-permute-start(bf16[4,2,48,768]{3,2,1,0:T(8,128)(2,1)} %dynamic-slice_bitcast_fusion.9), channel_id=1, source_target_pairs={{0,8},{8,0},{1,9},{9,1},{2,10},{10,2},{3,11},{11,3},{4,12},{12,4},... | collective-permute-start | bytes 1769480 | tf_op jit(solution)/shard_map/ppermute | solution.py:282
  337.9 29.7 %collective-permute-start.36 = (bf16[4,2,48,2304]{3,2,1,0:T(8,128)(2,1)S(1)}, bf16[4,2,48,2304]{3,2,1,0:T(8,128)(2,1)S(1)}, u32[]{:S(2)}, u32[]{:S(2)}) collective-permute-start(bf16[4,2,48,2304]{3,2,1,0:T(8,128)(2,1)S(1)} %dynamic-slice_bitcast_fusion.3), channel_id=1, source_target_pairs={{0,8},{8,0},{1,9},{9,1},{2,10},{10,2},{3,11},{11,3},{4,12},{12,4},... | collective-permute-start | bytes 5308424 | tf_op jit(solution)/shard_map/ppermute | solution.py:282
  339.2 28.0 %collective-permute-start.38 = (bf16[4,48,3072]{2,1,0:T(8,128)(2,1)S(1)}, bf16[4,48,3072]{2,1,0:T(8,128)(2,1)S(1)}, u32[]{:S(2)}, u32[]{:S(2)}) collective-permute-start(bf16[4,48,3072]{2,1,0:T(8,128)(2,1)S(1)} %dynamic-slice_bitcast_fusion.6), channel_id=1, source_target_pairs={{0,1},{1,0},{2,3},{3,2},{4,5},{5,4},{6,7},{7,6},{8,9},{9,8},{10,11... | collective-permute-start | bytes 3538952 | tf_op jit(solution)/shard_map/ppermute | solution.py:282
  369.6 18.9 %collective-permute-start.40 = (bf16[2,48,2304]{2,1,0:T(8,128)(2,1)S(1)}, bf16[2,48,2304]{2,1,0:T(8,128)(2,1)S(1)}, u32[]{:S(2)}, u32[]{:S(2)}) collective-permute-start(bf16[2,48,2304]{2,1,0:T(8,128)(2,1)S(1)} %dynamic-slice_bitcast_fusion.11), channel_id=1, source_target_pairs={{0,2},{1,3},{2,4},{3,5},{4,6},{5,7},{6,0},{7,1},{8,10},{9,11},{10,... | collective-permute-start | bytes 1327112 | tf_op jit(solution)/shard_map/ppermute | solution.py:287
  388.6 19.8 %collective-permute-start.41 = (bf16[192,768]{1,0:T(8,128)(2,1)S(1)}, bf16[192,768]{1,0:T(8,128)(2,1)S(1)}, u32[]{:S(2)}, u32[]{:S(2)}) collective-permute-start(bf16[192,768]{1,0:T(8,128)(2,1)S(1)} %fusion.61), channel_id=1, source_target_pairs={{0,2},{1,3},{2,4},{3,5},{4,6},{5,7},{6,0},{7,1},{8,10},{9,11},{10,... | collective-permute-start | bytes 884744 | tf_op jit(solution)/shard_map/ppermute | solution.py:287
  388.6 19.7 %collective-permute-start.42 = (bf16[48,3072]{1,0:T(8,128)(2,1)S(1)}, bf16[48,3072]{1,0:T(8,128)(2,1)S(1)}, u32[]{:S(2)}, u32[]{:S(2)}) collective-permute-start(bf16[48,3072]{1,0:T(8,128)(2,1)S(1)} %dynamic-slice_bitcast_fusion.15), channel_id=1, source_target_pairs={{0,2},{1,3},{2,4},{3,5},{4,6},{5,7},{6,0},{7,1},{8,10},{9,11},{10,... | collective-permute-start | bytes 884744 | tf_op jit(solution)/shard_map/ppermute | solution.py:287
  388.8 19.5 %collective-permute-start.43 = (bf16[48,768]{1,0:T(8,128)(2,1)S(1)}, bf16[48,768]{1,0:T(8,128)(2,1)S(1)}, u32[]{:S(2)}, u32[]{:S(2)}) collective-permute-start(bf16[48,768]{1,0:T(8,128)(2,1)S(1)} %dynamic-slice_bitcast_fusion.19), channel_id=1, source_target_pairs={{0,2},{1,3},{2,4},{3,5},{4,6},{5,7},{6,0},{7,1},{8,10},{9,11},{10,... | collective-permute-start | bytes 221192 | tf_op jit(solution)/shard_map/ppermute | solution.py:287
  391.4 23.7 %collective-permute-start.44 = (bf16[2,48,2304]{2,1,0:T(8,128)(2,1)S(1)}, bf16[2,48,2304]{2,1,0:T(8,128)(2,1)S(1)}, u32[]{:S(2)}, u32[]{:S(2)}) collective-permute-start(bf16[2,48,2304]{2,1,0:T(8,128)(2,1)S(1)} %fusion.52), channel_id=1, source_target_pairs={{0,2},{1,3},{2,4},{3,5},{4,6},{5,7},{6,0},{7,1},{8,10},{9,11},{10,... | collective-permute-start | bytes 1327112 | tf_op jit(solution)/shard_map/ppermute | solution.py:287
  393.8 21.4 %collective-permute-start.45 = (bf16[4,2,192,768]{3,2,0,1:T(8,128)(2,1)}, bf16[4,2,192,768]{3,2,0,1:T(8,128)(2,1)}, u32[]{:S(2)}, u32[]{:S(2)}) collective-permute-start(bf16[4,2,192,768]{3,2,0,1:T(8,128)(2,1)} %bitcast.332), channel_id=1, source_target_pairs={{0,8},{8,0},{1,9},{9,1},{2,10},{10,2},{3,11},{11,3},{4,12},{12,4},... | collective-permute-start | bytes 7077896 | tf_op jit(solution)/shard_map/ppermute | solution.py:282
  423.8 21.5 %collective-permute-start.48 = (bf16[2,48,2304]{2,1,0:T(8,128)(2,1)S(1)}, bf16[2,48,2304]{2,1,0:T(8,128)(2,1)S(1)}, u32[]{:S(2)}, u32[]{:S(2)}) collective-permute-start(bf16[2,48,2304]{2,1,0:T(8,128)(2,1)S(1)} %fusion.51), channel_id=1, source_target_pairs={{0,2},{1,3},{2,4},{3,5},{4,6},{5,7},{6,0},{7,1},{8,10},{9,11},{10,... | collective-permute-start | bytes 1327112 | tf_op jit(solution)/shard_map/ppermute | solution.py:287
  427.3 50.4 %collective-permute-start.52 = (bf16[4,192,768]{2,1,0:T(8,128)(2,1)S(1)}, bf16[4,192,768]{2,1,0:T(8,128)(2,1)}, u32[]{:S(2)}, u32[]{:S(2)}) collective-permute-start(bf16[4,192,768]{2,1,0:T(8,128)(2,1)S(1)} %dynamic-slice_bitcast_fusion.5), channel_id=1, source_target_pairs={{0,1},{1,0},{2,3},{3,2},{4,5},{5,4},{6,7},{7,6},{8,9},{9,8},{10,11... | collective-permute-start | bytes 3538952 | tf_op jit(solution)/shard_map/ppermute | solution.py:282
  428.3 51.0 %collective-permute-start.53 = (bf16[4,2,48,3072]{3,2,0,1:T(8,128)(2,1)}, bf16[4,2,48,3072]{3,2,0,1:T(8,128)(2,1)}, u32[]{:S(2)}, u32[]{:S(2)}) collective-permute-start(bf16[4,2,48,3072]{3,2,0,1:T(8,128)(2,1)} %bitcast.331), channel_id=1, source_target_pairs={{0,8},{8,0},{1,9},{9,1},{2,10},{10,2},{3,11},{11,3},{4,12},{12,4},... | collective-permute-start | bytes 7077896 | tf_op jit(solution)/shard_map/ppermute | solution.py:282
  472.4 16.7 %collective-permute-start.55 = (bf16[4,2,48,768]{3,2,0,1:T(8,128)(2,1)S(1)}, bf16[4,2,48,768]{3,2,0,1:T(8,128)(2,1)S(1)}, u32[]{:S(2)}, u32[]{:S(2)}) collective-permute-start(bf16[4,2,48,768]{3,2,0,1:T(8,128)(2,1)S(1)} %bitcast.371), channel_id=1, source_target_pairs={{0,8},{8,0},{1,9},{9,1},{2,10},{10,2},{3,11},{11,3},{4,12},{12,4},... | collective-permute-start | bytes 1769480 | tf_op jit(solution)/shard_map/ppermute | solution.py:282
  485.6 115.7 %collective-permute-start.87 = (bf16[192,768]{1,0:T(8,128)(2,1)S(1)}, bf16[192,768]{1,0:T(8,128)(2,1)S(1)}, u32[]{:S(2)}, u32[]{:S(2)}) collective-permute-start(bf16[192,768]{1,0:T(8,128)(2,1)S(1)} %fusion.63), channel_id=1, source_target_pairs={{0,16},{16,0},{1,17},{17,1},{2,18},{18,2},{3,19},{19,3},{4,20},{20... | collective-permute-start | bytes 884744 | tf_op jit(solution)/shard_map/ppermute | solution.py:370
  492.1 36.9 %collective-permute-start.54 = (bf16[192,768]{1,0:T(8,128)(2,1)S(1)}, bf16[192,768]{1,0:T(8,128)(2,1)S(1)}, u32[]{:S(2)}, u32[]{:S(2)}) collective-permute-start(bf16[192,768]{1,0:T(8,128)(2,1)S(1)} %dynamic-slice_bitcast_fusion.14), channel_id=1, source_target_pairs={{0,2},{1,3},{2,4},{3,5},{4,6},{5,7},{6,0},{7,1},{8,10},{9,11},{10,... | collective-permute-start | bytes 884744 | tf_op jit(solution)/shard_map/ppermute | solution.py:287
  494.4 39.5 %collective-permute-start.56 = (bf16[4,2,48,2304]{3,2,1,0:T(8,128)(2,1)S(1)}, bf16[4,2,48,2304]{3,2,1,0:T(8,128)(2,1)S(1)}, u32[]{:S(2)}, u32[]{:S(2)}) collective-permute-start(bf16[4,2,48,2304]{3,2,1,0:T(8,128)(2,1)S(1)} %dynamic-slice_bitcast_fusion.2), channel_id=1, source_target_pairs={{0,8},{8,0},{1,9},{9,1},{2,10},{10,2},{3,11},{11,3},{4,12},{12,4},... | collective-permute-start | bytes 5308424 | tf_op jit(solution)/shard_map/ppermute | solution.py:282
  494.4 28.4 %collective-permute-start.77 = (bf16[4,48,3072]{2,1,0:T(8,128)(2,1)S(1)}, bf16[4,48,3072]{2,1,0:T(8,128)(2,1)S(1)}, u32[]{:S(2)}, u32[]{:S(2)}) collective-permute-start(bf16[4,48,3072]{2,1,0:T(8,128)(2,1)S(1)} %dynamic-slice_bitcast_fusion.4), channel_id=1, source_target_pairs={{0,1},{1,0},{2,3},{3,2},{4,5},{5,4},{6,7},{7,6},{8,9},{9,8},{10,11... | collective-permute-start | bytes 3538952 | tf_op jit(solution)/shard_map/ppermute | solution.py:282
  503.1 129.1 %collective-permute-start.63 = (bf16[48,2304]{1,0:T(8,128)(2,1)S(1)}, bf16[48,2304]{1,0:T(8,128)(2,1)S(1)}, u32[]{:S(2)}, u32[]{:S(2)}) collective-permute-start(bf16[48,2304]{1,0:T(8,128)(2,1)S(1)} %fusion.78), channel_id=1, source_target_pairs={{0,16},{16,0},{1,17},{17,1},{2,18},{18,2},{3,19},{19,3},{4,20},{20... | collective-permute-start | bytes 663560 | tf_op jit(solution)/shard_map/ppermute | solution.py:370
  529.0 52.3 %collective-permute-start.82 = (bf16[48,3072]{1,0:T(8,128)(2,1)S(1)}, bf16[48,3072]{1,0:T(8,128)(2,1)S(1)}, u32[]{:S(2)}, u32[]{:S(2)}) collective-permute-start(bf16[48,3072]{1,0:T(8,128)(2,1)S(1)} %fusion.64), channel_id=1, source_target_pairs={{0,16},{16,0},{1,17},{17,1},{2,18},{18,2},{3,19},{19,3},{4,20},{20... | collective-permute-start | bytes 884744 | tf_op jit(solution)/shard_map/ppermute | solution.py:370
  544.5 16.9 %collective-permute-start.84 = (bf16[192,768]{1,0:T(8,128)(2,1)S(1)}, bf16[192,768]{1,0:T(8,128)(2,1)S(1)}, u32[]{:S(2)}, u32[]{:S(2)}) collective-permute-start(bf16[192,768]{1,0:T(8,128)(2,1)S(1)} %fusion.57), channel_id=1, source_target_pairs={{0,2},{1,3},{2,4},{3,5},{4,6},{5,7},{6,0},{7,1},{8,10},{9,11},{10,... | collective-permute-start | bytes 884744 | tf_op jit(solution)/shard_map/ppermute | solution.py:287
  581.3 50.8 %collective-permute-start.57 = (f32[512,768]{1,0:T(8,128)S(1)}, f32[512,768]{1,0:T(8,128)S(1)}, u32[]{:S(2)}, u32[]{:S(2)}) collective-permute-start(f32[512,768]{1,0:T(8,128)S(1)} %fusion.46), channel_id=1, source_target_pairs={{0,8},{8,0},{1,9},{9,1},{2,10},{10,2},{3,11},{11,3},{4,12},{12,4},... | collective-permute-start | bytes 4718600 | tf_op jit(solution)/shard_map/ppermute | solution.py:282
  608.0 15.6 %collective-permute-start.88 = (f32[192,768]{1,0:T(8,128)S(1)}, f32[192,768]{1,0:T(8,128)S(1)}, u32[]{:S(2)}, u32[]{:S(2)}) collective-permute-start(f32[192,768]{1,0:T(8,128)S(1)} %fusion.68), channel_id=1, source_target_pairs={{0,8},{8,0},{1,9},{9,1},{2,10},{10,2},{3,11},{11,3},{4,12},{12,4},... | collective-permute-start | bytes 1769480 | tf_op jit(solution)/shard_map/ppermute | solution.py:282
  608.6 14.4 %collective-permute-start.60 = (bf16[2,48,2304]{2,1,0:T(8,128)(2,1)S(1)}, bf16[2,48,2304]{2,1,0:T(8,128)(2,1)S(1)}, u32[]{:S(2)}, u32[]{:S(2)}) collective-permute-start(bf16[2,48,2304]{2,1,0:T(8,128)(2,1)S(1)} %fusion.49), channel_id=1, source_target_pairs={{0,2},{1,3},{2,4},{3,5},{4,6},{5,7},{6,0},{7,1},{8,10},{9,11},{10,... | collective-permute-start | bytes 1327112 | tf_op jit(solution)/shard_map/ppermute | solution.py:287
  (93 other events, 1114.9 us)
